TPU v7x, 32 devices: a whole 2x2x4 slice. The times are simulated.
32 devices in a mesh: dp: 4 (over y, core), expert: 8 (over z, x).
Axes of the slice: x: 2, y: 2, z: 4, core: 2. Of those that a mesh axis runs over, the one named last changes fastest.
Arguments:
- tokens: bfloat16 [4096, 2048], P(('dp', 'expert')), may hold values from -9 to 9
- out_grad: bfloat16 [4096, 2048], P(('dp', 'expert')), may hold values from -1.8 to 1.8
- probs: bfloat16 [4096, 8], P(('dp', 'expert')), may hold values from 0.019897461 to 0.5
- expert_ids: int32 [4096, 8], P(('dp', 'expert')), may hold values from 0 to 31, all different within a row; in each aligned block of 128 rows (0 to 127, 128 to 255, ...) at most 40 rows name the same one
- dropped: int32 [4096, 8], P(('dp', 'expert')), may hold values 0 or 1
- preacts: bfloat16 [4, 32, 320, 768], P('dp', 'expert'), may hold values from -6 to 6
- w_gu: bfloat16 [32, 2048, 768], P('expert', 'dp'), may hold values from -0.125 to 0.125
- w_down: bfloat16 [32, 384, 2048], P('expert', None, 'dp'), may hold values from -0.3125 to 0.3125
Outputs:
- tok_grad: bfloat16 [4096, 2048], P(('dp', 'expert'))
- prob_grad: bfloat16 [4096, 8], P(('dp', 'expert'))
- grad_gu: float32 [32, 2048, 768], P('expert', 'dp')
- grad_down: float32 [32, 384, 2048], P('expert', None, 'dp')
- mean_square: float32 [], replicated
Inputs may be any that keep to these rules, and one draw needn't show every extreme that they name: `expert_ids`: each row names 8 different experts. Within the rows of one device no expert is named more than 40 times, a bound that some block reaches in every draw.
All inputs are finite; a program needn't handle non-finite values. No bound on the sum of `dropped` on one device may be relied on, other than what follows from the above.
Results may differ from a plain program's by a relative error of at most 0.017.
Values may be sent and summed in bfloat16 or wider, within the bound.
A program may use at most 128 MiB of HBM per device.

v0:
```python
import jax
import jax.numpy as jnp
from jax import lax
from jax.sharding import PartitionSpec as P

FW = 384
EXPERTS = 32
CAP = 40


def slot_match(expert_ids, dropped, experts, capacity):
    tok_rows, top_k = expert_ids.shape
    flat_ids = expert_ids.reshape(-1)
    onehot = (flat_ids[:, None] == jnp.arange(experts, dtype=jnp.int32)[None, :]).astype(jnp.int32)
    before = jnp.cumsum(onehot, axis=0) - onehot
    position = jnp.sum(before * onehot, axis=1)
    slot_ids = flat_ids * capacity + position
    slot_ids = jnp.where(dropped.reshape(-1) == 0, slot_ids, -1).reshape(tok_rows, top_k)
    every_slot = jnp.arange(experts * capacity, dtype=jnp.int32)
    return (every_slot[:, None, None] == slot_ids[None, :, :]).astype(jnp.float32)


def body(tokens, out_grad, probs, expert_ids, dropped, preacts, w_gu, w_down):
    expert_count = lax.axis_size("expert")
    local_experts = EXPERTS // expert_count
    model_width = tokens.shape[1]
    matches = slot_match(expert_ids, dropped, EXPERTS, CAP)
    counts_bf = jnp.sum(matches, axis=2).astype(jnp.bfloat16)
    x_bins = jnp.dot(counts_bf, tokens, preferred_element_type=jnp.float32).astype(jnp.bfloat16)
    grad_bins = jnp.dot(counts_bf, out_grad, preferred_element_type=jnp.float32).astype(
        jnp.bfloat16
    )
    prob_bins = jnp.einsum("qtk,tk->q", matches, probs.astype(jnp.float32)).astype(jnp.bfloat16)
    x_in, grad_in, prob_in = (
        lax.all_to_all(
            x_bins.reshape(EXPERTS, CAP, model_width),
            "expert",
            split_axis=0,
            concat_axis=0,
            tiled=True,
        ),
        lax.all_to_all(
            grad_bins.reshape(EXPERTS, CAP, model_width),
            "expert",
            split_axis=0,
            concat_axis=0,
            tiled=True,
        ),
        lax.all_to_all(
            prob_bins.reshape(EXPERTS, CAP), "expert", split_axis=0, concat_axis=0, tiled=True
        ),
    )
    x_in = x_in.reshape(expert_count, local_experts, CAP, model_width)
    grad_in = grad_in.reshape(expert_count, local_experts, CAP, model_width)
    prob_in = prob_in.reshape(expert_count, local_experts, CAP)
    w_gu_full, w_down_full = (
        lax.all_gather(w_gu, "dp", axis=1, tiled=True),
        lax.all_gather(w_down, "dp", axis=2, tiled=True),
    )
    pre_acts = preacts.reshape(local_experts, expert_count, CAP, 2 * FW)
    proj = jnp.einsum("jecd,efd->ejcf", grad_in, w_down_full, preferred_element_type=jnp.float32)
    gate_pre = pre_acts[..., :FW].astype(jnp.float32)
    up_pre = pre_acts[..., FW:].astype(jnp.float32)
    sigmoid_a = jax.nn.sigmoid(gate_pre)
    silu_a = gate_pre * sigmoid_a
    hidden = silu_a * up_pre
    slot_prob = jnp.sum(hidden * proj, axis=-1).astype(jnp.bfloat16)
    weight_p = jnp.transpose(prob_in, (1, 0, 2)).astype(jnp.float32)[..., None]
    scaled = weight_p * proj
    dgu = jnp.concatenate(
        [scaled * up_pre * sigmoid_a * (1.0 + gate_pre * (1.0 - sigmoid_a)), scaled * silu_a],
        axis=-1,
    ).astype(jnp.bfloat16)
    hidden_p = (weight_p * hidden).astype(jnp.bfloat16)
    grad_down_term = jnp.einsum(
        "ejcf,jecd->efd", hidden_p, grad_in, preferred_element_type=jnp.float32
    )
    grad_gu_term = jnp.einsum("jecd,ejcf->edf", x_in, dgu, preferred_element_type=jnp.float32)
    grad_gu = lax.psum_scatter(
        grad_gu_term.astype(jnp.bfloat16), "dp", scatter_dimension=1, tiled=True
    ).astype(jnp.float32)
    grad_down = lax.psum_scatter(
        grad_down_term.astype(jnp.bfloat16), "dp", scatter_dimension=2, tiled=True
    ).astype(jnp.float32)
    grad_gu, grad_down = (grad_gu, grad_down)
    slot_grad = jnp.einsum(
        "ejcf,edf->jecd", dgu, w_gu_full, preferred_element_type=jnp.float32
    ).astype(jnp.bfloat16)
    prob_slot = jnp.transpose(slot_prob, (1, 0, 2))
    grad_back = lax.all_to_all(slot_grad, "expert", split_axis=0, concat_axis=1, tiled=True)
    prob_back = lax.all_to_all(prob_slot, "expert", split_axis=0, concat_axis=1, tiled=True)
    grad_flat = grad_back.reshape(EXPERTS * CAP, model_width)
    tok_grad = jnp.einsum(
        "qt,qd->td", counts_bf, grad_flat, preferred_element_type=jnp.float32
    ).astype(jnp.bfloat16)
    prob_grad = jnp.einsum("qtk,q->tk", matches, prob_back.reshape(-1).astype(jnp.float32)).astype(
        jnp.bfloat16
    )
    tok_grad, prob_grad = (tok_grad, prob_grad)
    partial_sq = jnp.sum(grad_gu * grad_gu) + jnp.sum(grad_down * grad_down)
    total = lax.psum(partial_sq, ("dp", "expert"))
    mean_square = total / (EXPERTS * 3 * model_width * FW)
    return (tok_grad, prob_grad, grad_gu, grad_down, mean_square)


def solution(mesh):
    return jax.shard_map(
        body,
        mesh=mesh,
        in_specs=(
            P(("dp", "expert"), None),
            P(("dp", "expert"), None),
            P(("dp", "expert"), None),
            P(("dp", "expert"), None),
            P(("dp", "expert"), None),
            P("dp", "expert", None, None),
            P("expert", "dp", None),
            P("expert", None, "dp"),
        ),
        out_specs=(
            P(("dp", "expert"), None),
            P(("dp", "expert"), None),
            P("expert", "dp", None),
            P("expert", None, "dp"),
            P(),
        ),
        check_vma=False,
    )
```

profile of v0, /device:TPU:0, one launch (start us, length us, event | category | flops | bytes accessed | tf_op | source)
XLA Modules:
  0.0 504.3 jit_solution(9027324610413388869)
XLA Ops:
  7.2 0.7 all-gather.3.cloned.1.call-update
  8.0 0.7 all-gather.5.cloned.1.call-update
  9.0 9.0 %reduce-window.6 = s32[32,8,128]{2,1,0:T(8,128)S(1)} reduce-window(s32[32,8,128]{2,1,0:T(8,128)S(1)} %fusion.26, s32[]{:T(128)} %constant.6.clone.1), window={size=1x1x128 pad=0_0x0_0x127_0}, to_apply=%region_0.0 | reduce-window | flops 4161536 | bytes 262148 | tf_op jit(solution)/shard_map/reduce-window
  18.7 0.9 iota_compare_fusion
  19.6 0.8 fusion.18
  20.4 0.7 all_to_all.26
  21.1 7.3 %all-to-all-start = ((bf16[8,4,40]{2,1,0:T(4,128)(2,1)}), bf16[8,4,40]{2,1,0:T(4,128)(2,1)S(1)}, u32[]{:S(2)}, u32[]{:S(2)}) async-start(bf16[8,4,40]{2,1,0:T(4,128)(2,1)} %all_to_all.26), calls=%async_computation | async-start | bytes 16384 | tf_op jit(solution)/shard_map/all_to_all | solution.py:49
  28.4 6.7 %convert_reduce_fusion = bf16[1280,128]{1,0:T(8,128)(2,1)S(1)} fusion(s32[128,8]{0,1:T(8,128)S(1)} %add_select_fusion), kind=kLoop, calls=%fused_computation.11 | loop fusion | flops 3768320 | bytes 331776 | tf_op jit(solution)/shard_map/reduce_sum | solution.py:28
  35.1 3.9 convolution_convert_fusion.1
  38.9 6.1 %all-to-all-start.1 = ((bf16[32,40,2048]{2,1,0:T(8,128)(2,1)}), bf16[32,40,2048]{2,1,0:T(8,128)(2,1)}, u32[]{:S(2)}, u32[]{:S(2)}) async-start(bf16[32,40,2048]{2,1,0:T(8,128)(2,1)} %bitcast.59), calls=%async_computation.1 | async-start | bytes 10485760 | tf_op jit(solution)/shard_map/all_to_all | solution.py:42
  45.1 0.2 reduce-scatter.5.cloned.1.call-start
  45.3 114.9 %all-to-all-done.1 = bf16[32,40,2048]{2,1,0:T(8,128)(2,1)} async-done(((bf16[32,40,2048]{2,1,0:T(8,128)(2,1)}), bf16[32,40,2048]{2,1,0:T(8,128)(2,1)}, u32[]{:S(2)}, u32[]{:S(2)}) %all-to-all-start.1) | async-done | bytes 5242912 | tf_op jit(solution)/shard_map/all_to_all | solution.py:42
  160.3 9.0 %bitcast_convert_fusion.1 = bf16[4,384,2048]{2,1,0:T(8,128)(2,1)} fusion(bf16[8,4,40,2048]{3,2,1,0:T(8,128)(2,1)} %bitcast.5, f32[4,8,40]{2,1,0:T(8,128)S(1)} %copy.75, bf16[4,8,40,768]{3,2,1,0:T(8,128)(2,1)S(1)} %bitcast.63), kind=kOutput, calls=%fused_computation.3 | convolution fusion | flops 2020835328 | bytes 13505536 | tf_op jit(solution)/shard_map/ejcf,jecd->efd/dot_general | solution.py:75
  169.3 1.0 copy-done.2
  170.3 3.9 convolution_convert_fusion
  174.3 4.9 all-to-all-start.4
  179.2 0.3 reduce-scatter.3.cloned.1.call-start
  179.5 9.8 %fusion.12 = (bf16[4,8,40,384]{3,2,1,0:T(8,128)(2,1)}, bf16[4,8,40,384]{3,2,1,0:T(8,128)(2,1)}, bf16[4,8,40]{2,1,0:T(8,128)(2,1)S(1)}) fusion(f32[4,8,40]{2,1,0:T(8,128)S(1)} %copy.75, bf16[4,8,40,768]{3,2,1,0:T(8,128)(2,1)S(1)} %bitcast.64, bf16[4,384,2048]{2,1,0:T(8,128)(2,1)} %all-gather.3.cloned.1.call-done, bf16[8,4,40,2048]{3,2,1,0:T(8,128)(2,1)} %bitcast.5), kind=kOutput, calls=%fused_computation.26 | convolution fusion | flops 2022603520 | bytes 15474176 | tf_op jit(solution)/shard_map/jecd,efd->ejcf/dot_general | solution.py:61
  189.3 104.5 %all-to-all-done.4 = bf16[32,40,2048]{2,1,0:T(8,128)(2,1)} async-done(((bf16[32,40,2048]{2,1,0:T(8,128)(2,1)}), bf16[32,40,2048]{2,1,0:T(8,128)(2,1)}, u32[]{:S(2)}, u32[]{:S(2)}) %all-to-all-start.4) | async-done | bytes 5242912 | tf_op jit(solution)/shard_map/all_to_all | solution.py:35
  293.7 11.9 %bitcast_convert_fusion = bf16[4,2048,768]{2,1,0:T(8,128)(2,1)} fusion(bf16[8,4,40,2048]{3,2,1,0:T(8,128)(2,1)} %bitcast.15, bf16[4,8,40,384]{3,2,1,0:T(8,128)(2,1)} %get-tuple-element.10, bf16[4,8,40,384]{3,2,1,0:T(8,128)(2,1)} %get-tuple-element.9), kind=kOutput, calls=%fused_computation | convolution fusion | flops 4036755456 | bytes 19791872 | tf_op jit(solution)/shard_map/jecd,ejcf->edf/dot_general | solution.py:78
  305.7 0.6 copy.78
  306.3 3.6 all-to-all-start.3
  309.9 16.6 %convert_bitcast_fusion = bf16[8,4,40,2048]{3,2,0,1:T(8,128)(2,1)} fusion(bf16[4,2048,768]{2,1,0:T(8,128)(2,1)} %all-gather.5.cloned.1.call-done, bf16[4,8,40,384]{3,2,1,0:T(8,128)(2,1)S(1)} %copy-done.8, bf16[4,8,40,384]{3,2,1,0:T(8,128)(2,1)S(1)} %copy-done.7), kind=kOutput, calls=%fused_computation.10 | convolution fusion | flops 4033085440 | bytes 19791872 | tf_op jit(solution)/shard_map/ejcf,edf->jecd/dot_general | solution.py:86
  326.5 5.7 %copy.77 = bf16[8,4,40,2048]{3,2,1,0:T(8,128)(2,1)} copy(bf16[8,4,40,2048]{3,2,0,1:T(8,128)(2,1)} %convert_bitcast_fusion) | data formatting | bytes 10485760 | tf_op jit(solution)/shard_map/convert_element_type | solution.py:88
  332.2 6.0 %all-to-all-start.2 = ((bf16[8,4,40,2048]{3,2,1,0:T(8,128)(2,1)}), bf16[8,4,40,2048]{3,2,1,0:T(8,128)(2,1)}, u32[]{:S(2)}, u32[]{:S(2)}) async-start(bf16[8,4,40,2048]{3,2,1,0:T(8,128)(2,1)} %copy.77), calls=%async_computation.2 | async-start | bytes 10485760 | tf_op jit(solution)/shard_map/all_to_all | solution.py:90
  338.2 4.2 select_reduce_fusion
  342.4 4.4 multiply_reduce_fusion.1
  346.9 57.1 %reduce-scatter.3.cloned.1.call-done = bf16[4,512,768]{2,1,0:T(8,128)(2,1)} async-done(((bf16[4,2048,768]{2,1,0:T(8,128)(2,1)}), bf16[4,512,768]{2,1,0:T(8,128)(2,1)}) %reduce-scatter.3.cloned.1.call-update) | async-done | bytes 3145744 | tf_op jit(solution)/shard_map/reduce_scatter | solution.py:79
  404.0 6.8 %multiply_reduce_fusion = (f32[]{:T(128)}, f32[4,512,768]{2,1,0:T(8,128)}) fusion(bf16[4,512,768]{2,1,0:T(8,128)(2,1)} %reduce-scatter.3.cloned.1.call-done), kind=kLoop, calls=%fused_computation.8 | loop fusion | flops 4718591 | bytes 9437188 | tf_op jit(solution)/shard_map/reduce_sum | solution.py:100
  412.1 42.0 %all-to-all-done.2 = bf16[8,4,40,2048]{3,2,1,0:T(8,128)(2,1)} async-done(((bf16[8,4,40,2048]{3,2,1,0:T(8,128)(2,1)}), bf16[8,4,40,2048]{3,2,1,0:T(8,128)(2,1)}, u32[]{:S(2)}, u32[]{:S(2)}) %all-to-all-start.2) | async-done | bytes 5242912 | tf_op jit(solution)/shard_map/all_to_all | solution.py:90
  454.1 4.2 convolution_convert_fusion.2
  458.2 37.8 %psum.7 = f32[]{:T(128)} all-reduce(f32[]{:T(128)S(6)} %add.23), channel_id=1, replica_groups=mesh['dp'=4,'expert'=8] {'dp','expert'}, use_global_device_ids=true, to_apply=%region_9.10 | all-reduce | flops 1 | bytes 8 | tf_op jit(solution)/shard_map/psum | solution.py:101
  (44 shorter events, 1.2 us)
Async XLA Ops:
  7.2 27.9 %copy-start = (bf16[128,2048]{1,0:T(8,128)(2,1)S(1)}, bf16[128,2048]{1,0:T(8,128)(2,1)}, u32[]{:S(2)}) copy-start(bf16[128,2048]{1,0:T(8,128)(2,1)} %param.9) | copy-start | bytes 1572868
  7.2 1.5 copy-start.3
  7.2 11.5 %copy-start.4 = (s32[128,8]{0,1:T(8,128)S(1)}, s32[128,8]{0,1:T(8,128)}, u32[]{:S(2)}) copy-start(s32[128,8]{0,1:T(8,128)} %param.12) | copy-start | bytes 12292
  7.2 172.3 %all-gather.3.cloned.1.call-start = ((), (), s32[]{:S(2)}) async-start(), calls=%async_computation.7 | async-start | bytes 7864320 | tf_op jit(solution)/shard_map/all_gather | solution.py:58
  7.9 11.6 %copy-start.6 = (bf16[128,8]{0,1:T(8,128)(2,1)S(1)}, bf16[128,8]{0,1:T(8,128)(2,1)}, u32[]{:S(2)}) copy-start(bf16[128,8]{0,1:T(8,128)(2,1)} %param.10) | copy-start | bytes 6148
  7.9 302.0 %all-gather.5.cloned.1.call-start = ((), (), s32[]{:S(2)}) async-start(), calls=%async_computation.8 | async-start | bytes 15728640 | tf_op jit(solution)/shard_map/all_gather | solution.py:57
  21.1 17.8 %all-to-all-start = ((bf16[8,4,40]{2,1,0:T(4,128)(2,1)}), bf16[8,4,40]{2,1,0:T(4,128)(2,1)S(1)}, u32[]{:S(2)}, u32[]{:S(2)}) async-start(bf16[8,4,40]{2,1,0:T(4,128)(2,1)} %all_to_all.26), calls=%async_computation | async-start | bytes 16384 | tf_op jit(solution)/shard_map/all_to_all | solution.py:49
  38.9 121.3 %copy-start.5 = (bf16[1,4,320,768]{3,2,1,0:T(8,128)(2,1)S(1)}, bf16[1,4,320,768]{3,2,1,0:T(8,128)(2,1)}, u32[]{:S(2)}) copy-start(bf16[1,4,320,768]{3,2,1,0:T(8,128)(2,1)} %param.13) | copy-start | bytes 5898244
  38.9 121.3 %all-to-all-start.1 = ((bf16[32,40,2048]{2,1,0:T(8,128)(2,1)}), bf16[32,40,2048]{2,1,0:T(8,128)(2,1)}, u32[]{:S(2)}, u32[]{:S(2)}) async-start(bf16[32,40,2048]{2,1,0:T(8,128)(2,1)} %bitcast.59), calls=%async_computation.1 | async-start | bytes 10485760 | tf_op jit(solution)/shard_map/all_to_all | solution.py:42
  45.1 297.4 %reduce-scatter.5.cloned.1.call-start = ((), (), s32[]{:S(2)}) async-start(), calls=%async_computation.10 | async-start | bytes 7864320 | tf_op jit(solution)/shard_map/reduce_scatter | solution.py:82
  169.3 1.0 copy-start.2
  174.3 119.4 %all-to-all-start.4 = ((bf16[32,40,2048]{2,1,0:T(8,128)(2,1)}), bf16[32,40,2048]{2,1,0:T(8,128)(2,1)}, u32[]{:S(2)}, u32[]{:S(2)}) async-start(bf16[32,40,2048]{2,1,0:T(8,128)(2,1)} %bitcast.58), calls=%async_computation.4 | async-start | bytes 10485760 | tf_op jit(solution)/shard_map/all_to_all | solution.py:35
  179.2 224.7 %reduce-scatter.3.cloned.1.call-start = ((), (), s32[]{:S(2)}) async-start(), calls=%async_computation.9 | async-start | bytes 15728640 | tf_op jit(solution)/shard_map/reduce_scatter | solution.py:79
  305.6 4.3 copy-start.7
  305.6 4.3 copy-start.8
  306.3 25.9 %all-to-all-start.3 = ((bf16[8,4,40]{2,1,0:T(4,128)(2,1)}), bf16[8,4,40]{2,1,0:T(4,128)(2,1)S(1)}, u32[]{:S(2)}, u32[]{:S(2)}) async-start(bf16[8,4,40]{2,1,0:T(4,128)(2,1)} %copy.78), calls=%async_computation.3 | async-start | bytes 16384 | tf_op jit(solution)/shard_map/all_to_all | solution.py:91
  332.2 121.9 %all-to-all-start.2 = ((bf16[8,4,40,2048]{3,2,1,0:T(8,128)(2,1)}), bf16[8,4,40,2048]{3,2,1,0:T(8,128)(2,1)}, u32[]{:S(2)}, u32[]{:S(2)}) async-start(bf16[8,4,40,2048]{3,2,1,0:T(8,128)(2,1)} %copy.77), calls=%async_computation.2 | async-start | bytes 10485760 | tf_op jit(solution)/shard_map/all_to_all | solution.py:90
  404.0 92.7 %copy-start.1 = (bf16[128,2048]{1,0:T(8,128)(2,1)S(1)}, bf16[128,2048]{1,0:T(8,128)(2,1)}, u32[]{:S(2)}) copy-start(bf16[128,2048]{1,0:T(8,128)(2,1)} %param.9) | copy-start | bytes 1572868
Sparse Core Ops, SparseCore 0:
  9.6 49.0 all-gather.2
  60.3 82.0 all-gather.4
  169.4 57.4 reduce-scatter.4
  305.8 98.1 reduce-scatter.2
where the time goes:
time: 506 us; the launch traced here: 504 us
  waiting for transfers between devices  320 us (63%)
  matrix products  60 us (12%)
  blocking collectives  37.8 us (7%)
  other arithmetic  32.2 us (6%)
  starting transfers between devices  28.5 us (6%)
  between operations  17.1 us (3%)
  local copies, waits for them, and re-layouts  8.81 us (2%)
    all_to_all x1, waiting for transfers between devices, body(): lax.all_to_all(grad_bins.reshape(EXPERTS, CAP, model_width), 'expert', sp...  115 us
    all_to_all x1, waiting for transfers between devices, body(): lax.all_to_all(x_bins.reshape(EXPERTS, CAP, model_width), 'expert', split...  104 us
    reduce_scatter x1, waiting for transfers between devices, body(): lax.psum_scatter(grad_gu_term.astype(jnp.bfloat16), 'dp', scatter_dimensi...  57.1 us
    all_to_all x1, waiting for transfers between devices, body(): lax.all_to_all(slot_grad, 'expert', split_axis=0, concat_axis=1, tiled=True)  42 us
    psum x1, blocking collectives, body(): total = lax.psum(partial_sq, ('dp', 'expert'))  37.8 us
    dot_general x1, matrix products, body(): jnp.einsum('ejcf,edf->jecd', dgu, w_gu_full, preferred_element_type=jnp.f...  16.6 us
    dot_general x1, matrix products, body(): jnp.einsum('jecd,ejcf->edf', x_in, dgu, preferred_element_type=jnp.float32)  11.9 us
    reduce_sum x2, other arithmetic, body(): partial_sq = jnp.sum(grad_gu * grad_gu) + jnp.sum(grad_down * grad_down)  11.2 us
  transfers between devices with their start and end apart: 9, of which 4 were waited for; matrix products, arithmetic and copies ran while one was open for 19% of the time, Pallas kernels for 0%

commit v1 on v0

v1 whole, which is shorter than its diff:
```python
import jax
import jax.numpy as jnp
from jax import lax
from jax.sharding import PartitionSpec as P

EXPERTS = 32
CAP = 40
BF = jnp.bfloat16
F32 = jnp.float32


def xor_permute(x, axis, bit):
    n = lax.axis_size(axis)
    return lax.ppermute(x, axis, [(a, a ^ bit) for a in range(n)])


def gather_rel(x, axis):
    n = lax.axis_size(axis)
    buf = x[None]
    bit = n // 2
    while bit:
        other = xor_permute(buf, axis, bit)
        buf = jnp.stack([buf, other], axis=1).reshape((-1,) + x.shape)
        bit //= 2
    return buf


def scatter_rel(x, axis, wire):
    n = lax.axis_size(axis)
    bit = 1
    while bit < n:
        got = xor_permute(x[1::2].astype(wire), axis, bit)
        x = x[0::2].astype(F32) + got.astype(F32)
        bit *= 2
    return x[0]


def swap_rel(pieces, axis):
    return [pieces[0]] + [xor_permute(pieces[r], axis, r) for r in range(1, len(pieces))]


def body(tokens, out_grad, probs, expert_ids, dropped, preacts, w_gu, w_down):
    n_dp, n_ex = lax.axis_size("dp"), lax.axis_size("expert")
    local = EXPERTS // n_ex
    rows, width = tokens.shape
    top = probs.shape[1]
    part = width // n_dp
    fw = w_down.shape[1]
    me, mine = lax.axis_index("dp"), lax.axis_index("expert")

    code = (expert_ids + EXPERTS * dropped).astype(F32)
    info = jnp.concatenate([code.T, probs.astype(F32).T], axis=0)
    info = lax.all_gather(info, ("dp", "expert"), axis=0, tiled=False)
    info = info.reshape(n_dp, n_ex, 2 * top, rows)

    def spread(x):
        pieces = [
            lax.dynamic_slice_in_dim(x, (me ^ r) * part, part, axis=1) for r in range(n_dp)
        ]
        got = jnp.stack(swap_rel(pieces, "dp"), axis=0)
        return lax.all_gather(got, "expert", axis=0, tiled=False)

    og = spread(out_grad)
    tk = spread(tokens)
    pre = gather_rel(preacts[0], "dp").reshape(n_dp, local, n_ex, CAP, 2 * fw)

    info = jnp.stack([info[me ^ r] for r in range(n_dp)], axis=1)
    code_all, prob_all = info[:, :, :top], info[:, :, top:]
    experts = (mine * local + jnp.arange(local)).astype(F32)[:, None, None]
    kept_k = (code_all[:, :, None] == experts).astype(F32)
    drop_k = (code_all[:, :, None] == experts + EXPERTS).astype(F32)
    kept = jnp.sum(kept_k, axis=3)
    here = kept + jnp.sum(drop_k, axis=3)
    prob_t = jnp.sum(kept_k * prob_all[:, :, None], axis=3)
    earlier = (jnp.arange(rows)[:, None] < jnp.arange(rows)[None, :]).astype(BF)
    pos = jnp.dot(
        here.astype(BF).reshape(-1, rows), earlier, preferred_element_type=F32
    ).reshape(here.shape)
    pos = jnp.where(kept > 0, pos, -1.0)
    hot = pos[:, :, :, None, :] == jnp.arange(CAP, dtype=F32)[:, None]
    ps = jnp.sum(jnp.where(hot, prob_t[:, :, :, None, :], 0.0), axis=-1)
    ps = jnp.transpose(ps, (1, 2, 0, 3))[..., None]
    pick = hot.astype(BF)

    gs = jnp.einsum("jreqt,jrtd->erjqd", pick, og, preferred_element_type=F32).astype(BF)
    proj = jnp.einsum("erjqd,efd->rejqf", gs, w_down, preferred_element_type=F32)
    own = scatter_rel(proj, "dp", BF)
    proj = gather_rel(own.astype(BF), "dp").astype(F32)

    gate, up = pre[..., :fw].astype(F32), pre[..., fw:].astype(F32)
    sig = jax.nn.sigmoid(gate)
    silu = gate * sig
    hidden = silu * up
    slot_prob = jnp.sum(hidden[0] * own, axis=-1).astype(BF).astype(F32)
    scaled = ps * proj
    dgu = jnp.concatenate(
        [scaled * up * sig * (1.0 + gate * (1.0 - sig)), scaled * silu], axis=-1
    ).astype(BF)
    hidden_p = (ps * hidden).astype(BF)

    slot_grad = jnp.einsum("rejqf,edf->erjqd", dgu, w_gu, preferred_element_type=F32).astype(BF)
    tok = jnp.einsum("jreqt,erjqd->jrtd", pick, slot_grad, preferred_element_type=F32).astype(BF)
    tok = lax.psum_scatter(tok, "expert", scatter_dimension=0, tiled=False)
    tok = swap_rel([tok[r] for r in range(n_dp)], "dp")
    tok = jnp.stack(tok, axis=0)
    tok_grad = jnp.concatenate([tok[me ^ p] for p in range(n_dp)], axis=-1)

    back = jnp.sum(
        jnp.where(hot[:, 0], jnp.transpose(slot_prob, (1, 0, 2))[..., None], 0.0), axis=2
    )
    back = lax.all_to_all(back, "expert", split_axis=0, concat_axis=0, tiled=True)
    back = back.reshape(EXPERTS, rows)
    named = code.T[:, None, :] == jnp.arange(EXPERTS, dtype=F32)[:, None]
    prob_grad = jnp.sum(jnp.where(named, back[None], 0.0), axis=1).T.astype(BF)

    xs = jnp.einsum("jreqt,jrtd->erjqd", pick, tk, preferred_element_type=F32).astype(BF)
    grad_down = jnp.einsum("rejqf,erjqd->efd", hidden_p, gs, preferred_element_type=F32)
    grad_gu = jnp.einsum("erjqd,rejqf->edf", xs, dgu, preferred_element_type=F32)
    square = jnp.sum(grad_gu * grad_gu) + jnp.sum(grad_down * grad_down)
    mean_square = lax.psum(square, ("dp", "expert")) / (EXPERTS * 3 * width * fw)
    return tok_grad, prob_grad, grad_gu, grad_down, mean_square


def solution(mesh):
    both = P(("dp", "expert"), None)
    weights = (P("expert", "dp", None), P("expert", None, "dp"))
    return jax.shard_map(
        body,
        mesh=mesh,
        in_specs=(both,) * 5 + (P("dp", "expert", None, None),) + weights,
        out_specs=(both, both) + weights + (P(),),
        check_vma=False,
    )
```

time: 506 us -> 407 us (0.80)
  waiting for transfers between devices: 320 us -> 157 us
  blocking collectives: 37.8 us -> 113 us
  matrix products: 60 us -> 47.6 us
  starting transfers between devices: 28.5 us -> 16.5 us
  local copies, waits for them, and re-layouts: 8.81 us -> 16.7 us
  other arithmetic: 32.2 us -> 37.9 us
    all_to_all x5 -> x1, waiting for transfers between devices: 261 us -> 0.01 us  [body(): lax.all_to_all(back, 'expert', split_axis=0, concat_axis=0, tiled=True)]
    ppermute x0 -> x15, waiting for transfers between devices: none -> 89.4 us  [xor_permute(): return lax.ppermute(x, axis, [(a, a ^ bit) for a in range(n)])]
    all_gather x0 -> x1, blocking collectives: none -> 72.8 us  [body(): info = lax.all_gather(info, ('dp', 'expert'), axis=0, tiled=False)]
    all_to_all x5 -> x1, starting transfers between devices: 27.9 us -> 3.54 us  [body(): lax.all_to_all(back, 'expert', split_axis=0, concat_axis=0, tiled=True)]
    convert_element_type x2 -> x6, other arithmetic: 0.02 us -> 15.3 us  [the longest x1 7.74 us: body(): hidden_p = (ps * hidden).astype(BF)]
    ppermute x0 -> x15, starting transfers between devices: none -> 12.6 us  [xor_permute(): return lax.ppermute(x, axis, [(a, a ^ bit) for a in range(n)])]
    dot_general x8, matrix products: 60 us -> 47.6 us  [the longest x1 12.6 us: body(): jnp.einsum('erjqd,rejqf->edf', xs, dgu, preferred_element_type=F32)]
    reduce_sum x4 -> x5, other arithmetic: 18 us -> 5.81 us  [the longest x1 2.23 us: body(): slot_prob = jnp.sum(hidden[0] * own, axis=-1).astype(BF).astype(F32)]
  transfers between devices with their start and end apart: 9 -> 19, of which waited for: 4 -> 11; matrix products, arithmetic and copies ran while one was open for 19% -> 22% of each run, Pallas kernels for 0% -> 0%
where the time goes in v1:
time: 407 us; the launch traced here: 406 us
  waiting for transfers between devices  157 us (39%)
  blocking collectives  113 us (28%)
  matrix products  47.6 us (12%)
  other arithmetic  37.9 us (9%)
  between operations  17.2 us (4%)
  local copies, waits for them, and re-layouts  16.7 us (4%)
  starting transfers between devices  16.5 us (4%)
    ppermute x15, waiting for transfers between devices, xor_permute(): return lax.ppermute(x, axis, [(a, a ^ bit) for a in range(n)])  89.4 us
    all_gather x1, blocking collectives, body(): info = lax.all_gather(info, ('dp', 'expert'), axis=0, tiled=False)  72.8 us
    reduce_scatter x1, waiting for transfers between devices, body(): tok = lax.psum_scatter(tok, 'expert', scatter_dimension=0, tiled=False)  64.8 us
    psum x1, blocking collectives, body(): lax.psum(square, ('dp', 'expert')) / (EXPERTS * 3 * width * fw)  40.3 us
    ppermute x15, starting transfers between devices, xor_permute(): return lax.ppermute(x, axis, [(a, a ^ bit) for a in range(n)])  12.6 us
    dot_general x1, matrix products, body(): jnp.einsum('erjqd,rejqf->edf', xs, dgu, preferred_element_type=F32)  12.6 us
    another operation x3, other arithmetic, gather_rel(): buf = jnp.stack([buf, other], axis=1).reshape((-1,) + x.shape)  11.1 us
    dot_general x1, matrix products, body(): jnp.einsum('rejqf,erjqd->efd', hidden_p, gs, preferred_element_type=F32)  8.32 us
  transfers between devices with their start and end apart: 19, of which 11 were waited for; matrix products, arithmetic and copies ran while one was open for 22% of the time, Pallas kernels for 0%

profile of v1, /device:TPU:0, one launch (start us, length us, event | category | flops | bytes accessed | tf_op | source)
XLA Modules:
  0.0 406.3 jit_solution(8541563286161192270)
XLA Ops:
  9.1 2.6 collective-permute-start.1
  11.7 4.3 %collective-permute-done.1 = bf16[128,512]{1,0:T(8,128)(2,1)S(1)} collective-permute-done((bf16[128,512]{1,0:T(8,128)(2,1)S(1)}, bf16[128,512]{1,0:T(8,128)(2,1)S(1)}, u32[]{:S(2)}, u32[]{:S(2)}) %collective-permute-start.1) | collective-permute-done | bytes 131104 | tf_op jit(solution)/shard_map/ppermute | solution.py:14
  16.0 2.3 collective-permute-done.2
  21.3 72.8 %all-gather = f32[512,128]{1,0:T(8,128)S(1)} all-gather(f32[16,128]{1,0:T(8,128)S(1)} %pad_maximum_fusion.9), channel_id=2, replica_groups=mesh['dp'=4,'expert'=8] {'dp','expert'}, dimensions={0}, use_global_device_ids=true | all-gather | bytes 270336 | tf_op jit(solution)/shard_map/all_gather | solution.py:53
  94.9 1.8 all-gather.6.cloned.1.call-done
  96.8 3.7 convert_bitcast_fusion.1
  100.5 5.7 %fusion.55 = (bf16[4,4,8,40,384]{4,3,2,0,1:T(8,128)(2,1)S(1)}, f32[4,4,8,40,384]{4,3,2,0,1:T(8,128)S(1)}) fusion(bf16[4,384,512]{2,1,0:T(8,128)(2,1)} %param.15, bf16[4,4,8,40,512]{4,3,0,2,1:T(8,128)(2,1)S(1)} %convert_bitcast_fusion.1), kind=kOutput, calls=%fused_computation.106 | convolution fusion | flops 2015232000 | bytes 18612224 | tf_op jit(solution)/shard_map/erjqd,efd->rejqf/dot_general | solution.py:86
  106.5 1.8 collective-permute-start.7
  108.3 2.2 collective-permute-done.3
  113.7 38.5 %collective-permute-done.7 = bf16[1,4,320,768]{3,2,1,0:T(8,128)(2,1)S(1)} collective-permute-done((bf16[1,4,320,768]{3,2,1,0:T(8,128)(2,1)S(1)}, bf16[1,4,320,768]{3,2,1,0:T(8,128)(2,1)S(1)}, u32[]{:S(2)}, u32[]{:S(2)}) %collective-permute-start.7) | collective-permute-done | bytes 1966112 | tf_op jit(solution)/shard_map/ppermute | solution.py:14
  152.2 3.5 fusion.37
  158.1 4.3 %collective-permute-done.12 = bf16[128,512]{1,0:T(8,128)(2,1)S(1)} collective-permute-done((bf16[128,512]{1,0:T(8,128)(2,1)S(1)}, bf16[128,512]{1,0:T(8,128)(2,1)S(1)}, u32[]{:S(2)}, u32[]{:S(2)}) %collective-permute-start.12) | collective-permute-done | bytes 131104 | tf_op jit(solution)/shard_map/ppermute | solution.py:14
  162.3 13.7 %collective-permute-done.13 = bf16[128,512]{1,0:T(8,128)(2,1)S(1)} collective-permute-done((bf16[128,512]{1,0:T(8,128)(2,1)S(1)}, bf16[128,512]{1,0:T(8,128)(2,1)S(1)}, u32[]{:S(2)}, u32[]{:S(2)}) %collective-permute-start.13) | collective-permute-done | bytes 131104 | tf_op jit(solution)/shard_map/ppermute | solution.py:14
  176.1 1.9 collective-permute-done.14
  179.1 2.2 fusion.48
  181.3 1.8 collective-permute-start.5
  183.1 22.2 %collective-permute-done.5 = bf16[1,4,8,40,384]{4,3,2,0,1:T(8,128)(2,1)S(1)} collective-permute-done((bf16[1,4,8,40,384]{4,3,2,0,1:T(8,128)(2,1)S(1)}, bf16[1,4,8,40,384]{4,3,2,0,1:T(8,128)(2,1)S(1)}, u32[]{:S(2)}, u32[]{:S(2)}) %collective-permute-start.5) | collective-permute-done | bytes 983072 | tf_op jit(solution)/shard_map/ppermute | solution.py:14
  207.8 5.9 %pad_maximum_fusion = bf16[2,2,4,320,768]{4,3,2,0,1:T(8,128)(2,1)} fusion(bf16[2,1,4,320,768]{4,3,2,0,1:T(8,128)(2,1)} %bitcast.30, bf16[2,1,4,320,768]{4,3,2,0,1:T(8,128)(2,1)S(1)} %copy-done.5), kind=kLoop, calls=%fused_computation.13 | loop fusion | flops 3932160 | bytes 15728640 | tf_op jit(solution)/shard_map/stack | solution.py:23
  213.7 7.1 %copy.52 = bf16[2,2,4,320,768]{4,3,1,0,2:T(8,128)(2,1)} copy(bf16[2,2,4,320,768]{4,3,2,0,1:T(8,128)(2,1)} %pad_maximum_fusion) | data formatting | bytes 15728640 | tf_op jit(solution)/shard_map/stack | solution.py:23
  220.8 5.3 %maximum_convert_fusion = f32[2,2,4,8,40,384]{5,4,3,2,0,1:T(8,128)} fusion(bf16[2,1,4,8,40,384]{5,4,3,2,0,1:T(8,128)(2,1)} %bitcast.24, bf16[2,1,4,8,40,384]{5,4,3,2,0,1:T(8,128)(2,1)S(1)} %get-tuple-element.16), kind=kLoop, calls=%fused_computation.33 | loop fusion | flops 3932160 | bytes 11796480 | tf_op jit(solution)/shard_map/convert_element_type | solution.py:88
  226.1 4.0 copy.51
  230.4 7.7 %multiply_convert_fusion = (bf16[4,4,8,40,384]{4,3,2,0,1:T(8,128)(2,1)}, f32[4,4,8,40,384]{4,3,2,0,1:T(8,128)}, bf16[4,4,8,40,384]{4,3,2,0,1:T(8,128)(2,1)S(1)}, bf16[4,4,8,40,384]{4,3,2,0,1:T(8,128)(2,1)}) fusion(f32[4,4,8,40]{3,2,0,1:T(8,128)S(1)} %copy.47, bf16[4,4,8,40,768]{4,3,2,0,1:T(8,128)(2,1)S(1)} %bitcast.111, f32[4,4,8,40,384]{4,3,2,0,1:T(8,128)S(1)} %bitcast.112), kind=kLoop, calls=%fused_computation.19 | loop fusion | flops 37355520 | bytes 35409920 | tf_op jit(solution)/shard_map/convert_element_type | solution.py:99
  238.2 7.6 %fusion.9 = bf16[4,4,8,40,512]{4,3,0,1,2:T(8,128)(2,1)S(1)} fusion(bf16[4,512,768]{2,1,0:T(8,128)(2,1)S(1)} %copy-done, bf16[4,4,8,40,384]{4,3,2,0,1:T(8,128)(2,1)S(1)} %get-tuple-element.12, bf16[4,4,8,40,384]{4,3,2,0,1:T(8,128)(2,1)} %get-tuple-element.13), kind=kOutput, calls=%fused_computation.17 | convolution fusion | flops 4042260480 | bytes 16252928 | tf_op jit(solution)/shard_map/rejqf,edf->erjqd/dot_general | solution.py:101
  245.7 3.4 bitcast_convert_fusion
  250.9 6.2 %convert_bitcast_fusion = bf16[4,4,8,40,512]{4,3,1,2,0:T(8,128)(2,1)} fusion(bf16[8,4,128,512,1]{3,2,1,0,4:T(8,128)(2,1)} %bitcast.129, f32[8,4,4,128]{3,2,1,0:T(4,128)S(1)} %copy.46), kind=kOutput, calls=%fused_computation.27 | convolution fusion | flops 674365440 | bytes 9502720 | tf_op jit(solution)/shard_map/jreqt,jrtd->erjqd/dot_general | solution.py:116
  257.1 2.2 fusion.38
  260.2 3.5 all-to-all-start
  263.8 12.6 %multiply_reduce_fusion = (f32[]{:T(128)}, f32[4,512,768]{2,1,0:T(8,128)}) fusion(bf16[4,4,8,40,512]{4,3,1,2,0:T(8,128)(2,1)} %convert_bitcast_fusion, bf16[4,4,8,40,384]{4,3,2,0,1:T(8,128)(2,1)} %copy-done.6, bf16[4,4,8,40,384]{4,3,2,0,1:T(8,128)(2,1)} %get-tuple-element.13), kind=kOutput, calls=%fused_computation.21 | convolution fusion | flops 4045406208 | bytes 19398660 | tf_op jit(solution)/shard_map/erjqd,rejqf->edf/dot_general | solution.py:118
  276.3 64.8 %reduce-scatter.2.cloned.1.call-done = bf16[1,4,128,512]{3,2,1,0:T(8,128)(2,1)} async-done(((bf16[8,4,128,512]{3,2,1,0:T(8,128)(2,1)}), bf16[1,4,128,512]{3,2,1,0:T(8,128)(2,1)}) %reduce-scatter.2.cloned.1.call-update) | async-done | bytes 524304 | tf_op jit(solution)/shard_map/reduce_scatter | solution.py:103
  341.1 1.8 slice_bitcast_fusion.4
  344.8 8.3 %multiply_reduce_fusion.1 = (f32[]{:T(128)}, f32[4,384,512]{2,1,0:T(8,128)}) fusion(bf16[4,4,8,40,512]{4,3,0,2,1:T(8,128)(2,1)} %copy-done.2, bf16[4,4,8,40,384]{4,3,2,0,1:T(8,128)(2,1)} %get-tuple-element.8), kind=kOutput, calls=%fused_computation.38 | convolution fusion | flops 2014838784 | bytes 12320772 | tf_op jit(solution)/shard_map/rejqf,erjqd->efd/dot_general | solution.py:117
  354.4 40.3 %psum.7 = f32[]{:T(128)} all-reduce(f32[]{:T(128)S(6)} %add.99), channel_id=1, replica_groups=mesh['dp'=4,'expert'=8] {'dp','expert'}, use_global_device_ids=true, to_apply=%region_10.11 | all-reduce | flops 1 | bytes 8 | tf_op jit(solution)/shard_map/psum | solution.py:120
  (82 shorter events, 23.1 us)
Async XLA Ops:
  7.2 231.0 %copy-start = (bf16[4,512,768]{2,1,0:T(8,128)(2,1)S(1)}, bf16[4,512,768]{2,1,0:T(8,128)(2,1)}, u32[]{:S(2)}) copy-start(bf16[4,512,768]{2,1,0:T(8,128)(2,1)} %param.14) | copy-start | bytes 9437188
  7.2 89.6 %all-gather.6.cloned.1.call-start = ((), (), s32[]{:S(2)}) async-start(), calls=%async_computation.3 | async-start | bytes 4718592 | tf_op jit(solution)/shard_map/all_gather | solution.py:61
  8.6 3.2 collective-permute-start
  9.1 6.9 %collective-permute-start.1 = (bf16[128,512]{1,0:T(8,128)(2,1)S(1)}, bf16[128,512]{1,0:T(8,128)(2,1)S(1)}, u32[]{:S(2)}, u32[]{:S(2)}) collective-permute-start(bf16[128,512]{1,0:T(8,128)(2,1)S(1)} %get-tuple-element.33), channel_id=1, source_target_pairs={{0,16},{8,24},{16,0},{24,8},{1,17},{9,25},{17,1},{25,9},{2,18},{10... | collective-permute-start | bytes 393224 | tf_op jit(solution)/shard_map/ppermute | solution.py:14
  11.7 6.6 %collective-permute-start.2 = (bf16[128,512]{1,0:T(8,128)(2,1)S(1)}, bf16[128,512]{1,0:T(8,128)(2,1)S(1)}, u32[]{:S(2)}, u32[]{:S(2)}) collective-permute-start(bf16[128,512]{1,0:T(8,128)(2,1)S(1)} %get-tuple-element.32), channel_id=1, source_target_pairs={{0,24},{8,16},{16,8},{24,0},{1,25},{9,17},{17,9},{25,1},{2,26},{10... | collective-permute-start | bytes 393224 | tf_op jit(solution)/shard_map/ppermute | solution.py:14
  19.2 231.7 %all-gather.8.cloned.1.call-start = ((), (), s32[]{:S(2)}) async-start(), calls=%async_computation.4 | async-start | bytes 4718592 | tf_op jit(solution)/shard_map/all_gather | solution.py:61
  20.7 0.6 copy-start.9
  100.5 5.7 %copy-start.2 = (bf16[4,4,8,40,512]{4,3,0,2,1:T(8,128)(2,1)}, bf16[4,4,8,40,512]{4,3,0,2,1:T(8,128)(2,1)S(1)}, u32[]{:S(2)}) copy-start(bf16[4,4,8,40,512]{4,3,0,2,1:T(8,128)(2,1)S(1)} %convert_bitcast_fusion.1) | copy-start | bytes 15728644
  100.5 6.0 %copy-start.7 = (bf16[1,4,320,768]{3,2,1,0:T(8,128)(2,1)S(1)}, bf16[1,4,320,768]{3,2,1,0:T(8,128)(2,1)}, u32[]{:S(2)}) copy-start(bf16[1,4,320,768]{3,2,1,0:T(8,128)(2,1)} %param.13) | copy-start | bytes 5898244
  106.4 4.0 collective-permute-start.3
  106.5 45.7 %collective-permute-start.7 = (bf16[1,4,320,768]{3,2,1,0:T(8,128)(2,1)S(1)}, bf16[1,4,320,768]{3,2,1,0:T(8,128)(2,1)S(1)}, u32[]{:S(2)}, u32[]{:S(2)}) collective-permute-start(bf16[1,4,320,768]{3,2,1,0:T(8,128)(2,1)S(1)} %copy-done.7), channel_id=1, source_target_pairs={{0,16},{8,24},{16,0},{24,8},{1,17},{9,25},{17,1},{25,9},{2,18},{10... | collective-permute-start | bytes 5898248 | tf_op jit(solution)/shard_map/ppermute | solution.py:14
  110.8 44.9 %copy-start.3 = (f32[2,4,8,40,384]{4,3,2,0,1:T(8,128)}, f32[2,4,8,40,384]{4,3,2,0,1:T(8,128)S(1)}, u32[]{:S(2)}) copy-start(f32[2,4,8,40,384]{4,3,2,0,1:T(8,128)S(1)} %convert_add_fusion) | copy-start | bytes 11796484
  112.0 67.1 %collective-permute-start.4 = (bf16[1,4,8,40,384]{4,3,2,0,1:T(8,128)(2,1)}, bf16[1,4,8,40,384]{4,3,2,0,1:T(8,128)(2,1)}, u32[]{:S(2)}, u32[]{:S(2)}) collective-permute-start(bf16[1,4,8,40,384]{4,3,2,0,1:T(8,128)(2,1)} %slice.104), channel_id=1, source_target_pairs={{0,16},{8,24},{16,0},{24,8},{1,17},{9,25},{17,1},{25,9},{2,18},{10... | collective-permute-start | bytes 2949128 | tf_op jit(solution)/shard_map/ppermute | solution.py:14
  152.2 3.5 copy-start.8
  155.7 52.0 %collective-permute-start.8 = (bf16[2,4,320,768]{3,2,1,0:T(8,128)(2,1)}, bf16[2,4,320,768]{3,2,1,0:T(8,128)(2,1)}, u32[]{:S(2)}, u32[]{:S(2)}) collective-permute-start(bf16[2,4,320,768]{3,2,1,0:T(8,128)(2,1)} %get-tuple-element.15), channel_id=1, source_target_pairs={{0,8},{8,0},{16,24},{24,16},{1,9},{9,1},{17,25},{25,17},{2,10},{10... | collective-permute-start | bytes 11796488 | tf_op jit(solution)/shard_map/ppermute | solution.py:14
  155.8 6.5 %collective-permute-start.12 = (bf16[128,512]{1,0:T(8,128)(2,1)S(1)}, bf16[128,512]{1,0:T(8,128)(2,1)S(1)}, u32[]{:S(2)}, u32[]{:S(2)}) collective-permute-start(bf16[128,512]{1,0:T(8,128)(2,1)S(1)} %get-tuple-element.19), channel_id=1, source_target_pairs={{0,8},{8,0},{16,24},{24,16},{1,9},{9,1},{17,25},{25,17},{2,10},{10... | collective-permute-start | bytes 393224 | tf_op jit(solution)/shard_map/ppermute | solution.py:14
  156.4 19.7 %collective-permute-start.13 = (bf16[128,512]{1,0:T(8,128)(2,1)S(1)}, bf16[128,512]{1,0:T(8,128)(2,1)S(1)}, u32[]{:S(2)}, u32[]{:S(2)}) collective-permute-start(bf16[128,512]{1,0:T(8,128)(2,1)S(1)} %get-tuple-element.21), channel_id=1, source_target_pairs={{0,16},{8,24},{16,0},{24,8},{1,17},{9,25},{17,1},{25,9},{2,18},{10... | collective-permute-start | bytes 393224 | tf_op jit(solution)/shard_map/ppermute | solution.py:14
  158.1 19.9 %collective-permute-start.14 = (bf16[128,512]{1,0:T(8,128)(2,1)S(1)}, bf16[128,512]{1,0:T(8,128)(2,1)S(1)}, u32[]{:S(2)}, u32[]{:S(2)}) collective-permute-start(bf16[128,512]{1,0:T(8,128)(2,1)S(1)} %get-tuple-element.20), channel_id=1, source_target_pairs={{0,24},{8,16},{16,8},{24,0},{1,25},{9,17},{17,9},{25,1},{2,26},{10... | collective-permute-start | bytes 393224 | tf_op jit(solution)/shard_map/ppermute | solution.py:14
  178.8 162.2 %reduce-scatter.2.cloned.1.call-start = ((), (), s32[]{:S(2)}) async-start(), calls=%async_computation.2 | async-start | bytes 4718592 | tf_op jit(solution)/shard_map/reduce_scatter | solution.py:103
  179.1 28.7 %copy-start.5 = (bf16[2,1,4,320,768]{4,3,2,0,1:T(8,128)(2,1)S(1)}, bf16[2,1,4,320,768]{4,3,2,0,1:T(8,128)(2,1)}, u32[]{:S(2)}) copy-start(bf16[2,1,4,320,768]{4,3,2,0,1:T(8,128)(2,1)} %get-tuple-element.14) | copy-start | bytes 11796484
  181.3 24.0 %collective-permute-start.5 = (bf16[1,4,8,40,384]{4,3,2,0,1:T(8,128)(2,1)S(1)}, bf16[1,4,8,40,384]{4,3,2,0,1:T(8,128)(2,1)S(1)}, u32[]{:S(2)}, u32[]{:S(2)}) collective-permute-start(bf16[1,4,8,40,384]{4,3,2,0,1:T(8,128)(2,1)S(1)} %fusion.48), channel_id=1, source_target_pairs={{0,16},{8,24},{16,0},{24,8},{1,17},{9,25},{17,1},{25,9},{2,18},{10... | collective-permute-start | bytes 2949128 | tf_op jit(solution)/shard_map/ppermute | solution.py:14
  206.9 13.9 %collective-permute-start.6 = (bf16[2,4,8,40,384]{4,3,2,1,0:T(8,128)(2,1)}, bf16[2,4,8,40,384]{4,3,2,1,0:T(8,128)(2,1)}, u32[]{:S(2)}, u32[]{:S(2)}) collective-permute-start(bf16[2,4,8,40,384]{4,3,2,1,0:T(8,128)(2,1)} %get-tuple-element.17), channel_id=1, source_target_pairs={{0,8},{8,0},{16,24},{24,16},{1,9},{9,1},{17,25},{25,17},{2,10},{10... | collective-permute-start | bytes 5898248 | tf_op jit(solution)/shard_map/ppermute | solution.py:14
  220.8 9.3 %slice-start = ((s8[7864320]{0:T(1024)(128)(4,1)}), s8[4194304]{0:T(1024)(128)(4,1)S(1)}, s32[]{:S(2)}) async-start(s8[7864320]{0:T(1024)(128)(4,1)} %bitcast.109), calls=%async_computation.5 | async-start | bytes 8388608
  226.1 4.3 %slice-start.1 = ((s8[7864320]{0:T(1024)(128)(4,1)}), s8[3670016]{0:T(1024)(128)(4,1)S(1)}, s32[]{:S(2)}) async-start(s8[7864320]{0:T(1024)(128)(4,1)} %bitcast.109), calls=%async_computation.6 | async-start | bytes 7340032
  238.2 7.6 %copy-start.6 = (bf16[4,4,8,40,384]{4,3,2,0,1:T(8,128)(2,1)}, bf16[4,4,8,40,384]{4,3,2,0,1:T(8,128)(2,1)S(1)}, u32[]{:S(2)}) copy-start(bf16[4,4,8,40,384]{4,3,2,0,1:T(8,128)(2,1)S(1)} %get-tuple-element.12) | copy-start | bytes 11796484
  250.9 6.2 %copy-start.4 = (f32[2,4,8,40,384]{4,3,2,0,1:T(8,128)S(1)}, f32[2,4,8,40,384]{4,3,2,0,1:T(8,128)}, u32[]{:S(2)}) copy-start(f32[2,4,8,40,384]{4,3,2,0,1:T(8,128)} %copy-done.3) | copy-start | bytes 11796484
  260.2 135.2 %all-to-all-start = ((f32[8,4,128]{2,1,0:T(4,128)}), f32[8,4,128]{2,1,0:T(4,128)S(1)}, u32[]{:S(2)}, u32[]{:S(2)}) async-start(f32[8,4,128]{2,1,0:T(4,128)} %select_reduce_fusion.1), calls=%async_computation.1 | async-start | bytes 32768 | tf_op jit(solution)/shard_map/all_to_all | solution.py:111
  342.9 53.8 %collective-permute-start.9 = (bf16[128,512]{1,0:T(8,128)(2,1)}, bf16[128,512]{1,0:T(8,128)(2,1)S(1)}, u32[]{:S(2)}, u32[]{:S(2)}) collective-permute-start(bf16[128,512]{1,0:T(8,128)(2,1)} %get-tuple-element.29), channel_id=1, source_target_pairs={{0,8},{8,0},{16,24},{24,16},{1,9},{9,1},{17,25},{25,17},{2,10},{10... | collective-permute-start | bytes 393224 | tf_op jit(solution)/shard_map/ppermute | solution.py:14
  342.9 53.8 %collective-permute-start.10 = (bf16[128,512]{1,0:T(8,128)(2,1)}, bf16[128,512]{1,0:T(8,128)(2,1)}, u32[]{:S(2)}, u32[]{:S(2)}) collective-permute-start(bf16[128,512]{1,0:T(8,128)(2,1)} %get-tuple-element.28), channel_id=1, source_target_pairs={{0,16},{8,24},{16,0},{24,8},{1,17},{9,25},{17,1},{25,9},{2,18},{10... | collective-permute-start | bytes 393224 | tf_op jit(solution)/shard_map/ppermute | solution.py:14
  344.4 52.3 %collective-permute-start.11 = (bf16[128,512]{1,0:T(8,128)(2,1)S(1)}, bf16[128,512]{1,0:T(8,128)(2,1)}, u32[]{:S(2)}, u32[]{:S(2)}) collective-permute-start(bf16[128,512]{1,0:T(8,128)(2,1)S(1)} %get-tuple-element.27), channel_id=1, source_target_pairs={{0,24},{8,16},{16,8},{24,0},{1,25},{9,17},{17,9},{25,1},{2,26},{10... | collective-permute-start | bytes 393224 | tf_op jit(solution)/shard_map/ppermute | solution.py:14
  344.8 53.9 %copy-start.1 = (bf16[4,512,768]{2,1,0:T(8,128)(2,1)S(1)}, bf16[4,512,768]{2,1,0:T(8,128)(2,1)}, u32[]{:S(2)}) copy-start(bf16[4,512,768]{2,1,0:T(8,128)(2,1)} %param.14) | copy-start | bytes 9437188
Sparse Core Ops, SparseCore 0:
  19.3 77.4 all-gather.5
  179.0 71.8 all-gather.7
  254.5 86.4 reduce-scatter.1

commit v2 on v1

--- a/solution.py
+++ b/solution.py
@@ -1,6 +1,10 @@
+import functools
+
 import jax
 import jax.numpy as jnp
 from jax import lax
+from jax.experimental import pallas as pl
+from jax.experimental.pallas import tpu as pltpu
 from jax.sharding import PartitionSpec as P
 
 EXPERTS = 32
@@ -25,18 +29,330 @@
     return buf
 
 
-def scatter_rel(x, axis, wire):
-    n = lax.axis_size(axis)
-    bit = 1
-    while bit < n:
-        got = xor_permute(x[1::2].astype(wire), axis, bit)
-        x = x[0::2].astype(F32) + got.astype(F32)
-        bit *= 2
-    return x[0]
-
-
 def swap_rel(pieces, axis):
     return [pieces[0]] + [xor_permute(pieces[r], axis, r) for r in range(1, len(pieces))]
+
+
+def remote(src, dst, sems, slot, axis, peer):
+    return pltpu.make_async_remote_copy(
+        src_ref=src,
+        dst_ref=dst,
+        send_sem=sems.at[(0,) + slot],
+        recv_sem=sems.at[(1,) + slot],
+        device_id={axis: peer},
+        device_id_type=pl.DeviceIdType.MESH,
+    )
+
+
+def greet(n_ex, n_dp, with_dp):
+    j = lax.axis_index("expert")
+    lines = n_ex // 2
+    z = j // 2
+    barrier = pltpu.get_barrier_semaphore()
+
+    def signal(axis, peer):
+        pl.semaphore_signal(
+            barrier, inc=1, device_id={axis: peer}, device_id_type=pl.DeviceIdType.MESH
+        )
+
+    count = 1
+    signal("expert", z * 2 + 1 - j % 2)
+
+    @pl.when(z > 0)
+    def _():
+        signal("expert", j - 2)
+
+    @pl.when(z < lines - 1)
+    def _():
+        signal("expert", j + 2)
+
+    if with_dp:
+        me = lax.axis_index("dp")
+        bit = 1
+        while bit < n_dp:
+            signal("dp", flip(me, bit))
+            count += 1
+            bit *= 2
+    count += (z + lines - 1) // lines + (2 * lines - 2 - z) // lines
+    pl.semaphore_wait(barrier, count)
+
+
+def flip(me, bit):
+    return me + bit - 2 * bit * ((me // bit) % 2)
+
+
+def expert_gather(n_ex, pairs, sems, local_sems):
+    j = lax.axis_index("expert")
+    lines = n_ex // 2
+    z, x = j // 2, j % 2
+    partner = z * 2 + 1 - x
+    todo = []
+
+    def up(a, s):
+        i, o = pairs[a]
+        b = (z - s) * 2 + x
+        return remote(i if s == 0 else o.at[b], o.at[b], sems, (a, 0, s), "expert", j + 2)
+
+    def down(a, s):
+        i, o = pairs[a]
+        b = (z + s) * 2 + x
+        return remote(i if s == 0 else o.at[b], o.at[b], sems, (a, 1, s), "expert", j - 2)
+
+    def across(a, z_of, first, s, side):
+        i, o = pairs[a]
+        b = z_of * 2 + x
+        return remote(i if first else o.at[b], o.at[b], sems, (a, 2 + side, s), "expert", partner)
+
+    def landed(a, b, kind, s):
+        i, o = pairs[a]
+        return remote(i, o.at[b], sems, (a, kind, s), "expert", partner)
+
+    def begin():
+        for a, (i, o) in enumerate(pairs):
+            pltpu.make_async_copy(i, o.at[j], local_sems.at[a]).start()
+
+            @pl.when(z < lines - 1)
+            def _():
+                up(a, 0).start()
+
+            @pl.when(z > 0)
+            def _():
+                down(a, 0).start()
+
+            across(a, z, True, 0, 0).start()
+
+    def step(s):
+        for a in range(len(pairs)):
+
+            @pl.when(z - 1 - s >= 0)
+            def _():
+                landed(a, (z - 1 - s) * 2 + x, 0, s).wait_recv()
+                if s + 1 < lines - 1:
+
+                    @pl.when(z < lines - 1)
+                    def _():
+                        up(a, s + 1).start()
+
+                across(a, z - 1 - s, False, s + 1, 0).start()
+
+            @pl.when(z + 1 + s < lines)
+            def _():
+                landed(a, (z + 1 + s) * 2 + x, 1, s).wait_recv()
+                if s + 1 < lines - 1:
+
+                    @pl.when(z > 0)
+                    def _():
+                        down(a, s + 1).start()
+
+                across(a, z + 1 + s, False, s + 1, 1).start()
+
+    def finish():
+        for a, (i, o) in enumerate(pairs):
+            pltpu.make_async_copy(i, o.at[j], local_sems.at[a]).wait()
+            landed(a, partner, 2, 0).wait_recv()
+            across(a, z, True, 0, 0).wait_send()
+            for s in range(lines - 1):
+
+                @pl.when((z - s >= 0) & (z < lines - 1))
+                def _():
+                    up(a, s).wait_send()
+
+                @pl.when((z + s < lines) & (z > 0))
+                def _():
+                    down(a, s).wait_send()
+
+                @pl.when(z - 1 - s >= 0)
+                def _():
+                    across(a, z - 1 - s, False, s + 1, 0).wait_send()
+                    landed(a, (z - 1 - s) * 2 + 1 - x, 2, s + 1).wait_recv()
+
+                @pl.when(z + 1 + s < lines)
+                def _():
+                    across(a, z + 1 + s, False, s + 1, 1).wait_send()
+                    landed(a, (z + 1 + s) * 2 + 1 - x, 3, s + 1).wait_recv()
+
+    todo.append(begin)
+    for s in range(lines - 1):
+        todo.append(functools.partial(step, s))
+    todo.append(finish)
+    return todo
+
+
+def dp_gather(n_dp, own, out, sems, chunks):
+    me = lax.axis_index("dp")
+    bits = []
+    bit = n_dp // 2
+    while bit:
+        bits.append(bit)
+        bit //= 2
+    size = out.shape[1] // chunks
+
+    def copy(level, r, c):
+        rows = pl.ds(c * size, size)
+        src = own.at[rows] if r == 0 else out.at[r, rows]
+        bit = bits[level]
+        return remote(src, out.at[r + bit, rows], sems, (level, r // (2 * bit), c), "dp", flip(me, bit))
+
+    def held(level):
+        return range(0, n_dp, 2 * bits[level])
+
+    def send(level, c):
+        if level:
+            for r in held(level - 1):
+                copy(level - 1, r, c).wait_recv()
+        for r in held(level):
+            copy(level, r, c).start()
+
+    def finish():
+        for c in range(chunks):
+            for r in held(len(bits) - 1):
+                copy(len(bits) - 1, r, c).wait_recv()
+            for level in range(len(bits)):
+                for r in held(level):
+                    copy(level, r, c).wait_send()
+
+    return send, finish, len(bits)
+
+
+def first_kernel(n_ex, n_dp, og, info, pre, og_all, info_all, pre_all, sems, local_sems, dp_sems, dp_local):
+    greet(n_ex, n_dp, True)
+    todo = expert_gather(n_ex, [(info, info_all), (og, og_all)], sems, local_sems)
+    send, finish, levels = dp_gather(n_dp, pre, pre_all, dp_sems, 2)
+    keep = pltpu.make_async_copy(pre, pre_all.at[0], dp_local)
+    todo[0]()
+    for c in range(2):
+        send(0, c)
+    keep.start()
+    todo[1]()
+    for t in todo[2:-1]:
+        t()
+    for level in range(1, levels):
+        for c in range(2):
+            send(level, c)
+    todo[-1]()
+    finish()
+    keep.wait()
+
+
+def second_kernel(n_ex, n_dp, chunks, tk, part, tk_all, own_out, proj_all, *scratch):
+    sems, local_sems, dp_sems, sum_sems = scratch[:4]
+    scratch = scratch[4:]
+    levels = len(scratch) // 2
+    got, acc = scratch[:levels], (part,) + scratch[levels:]
+    me = lax.axis_index("dp")
+    size = own_out.shape[0] // chunks
+    greet(n_ex, n_dp, True)
+    todo = expert_gather(n_ex, [(tk, tk_all)], sems, local_sems)
+    send, finish, gather_levels = dp_gather(n_dp, proj_all.at[0], proj_all, dp_sems, chunks)
+
+    def copy(level, k, c):
+        rows = pl.ds(c * size, size)
+        return remote(
+            acc[level].at[2 * k + 1, rows], got[level].at[k, rows], sums(level), (k, c), "dp", flip(me, 1 << level)
+        )
+
+    def sums(level):
+        return sum_sems.at[level]
+
+    def count(level):
+        return n_dp >> (level + 1)
+
+    def reduce(level, c):
+        rows = pl.ds(c * size, size)
+        for k in range(count(level)):
+            copy(level, k, c).wait_recv()
+            total = acc[level][2 * k, rows, :].astype(F32) + got[level][k, rows, :].astype(F32)
+            if level + 1 < levels:
+                acc[level + 1][k, rows, :] = total.astype(BF)
+            else:
+                own_out[rows, :] = total
+                proj_all[0, rows, :] = total.astype(BF)
+        if level + 1 < levels:
+            for k in range(count(level + 1)):
+                copy(level + 1, k, c).start()
+        else:
+            send(0, c)
+
+    for c in range(chunks):
+        for k in range(count(0)):
+            copy(0, k, c).start()
+    todo[0]()
+    rest = list(todo[1:-1])
+    for level in range(levels):
+        for c in range(chunks):
+            reduce(level, c)
+            if level == levels - 1 and c % 2 and rest:
+                rest.pop(0)()
+    for level in range(1, gather_levels):
+        for c in range(chunks):
+            send(level, c)
+            if rest:
+                rest.pop(0)()
+    for t in rest:
+        t()
+    todo[-1]()
+    finish()
+    for level in range(levels):
+        for k in range(count(level)):
+            for c in range(chunks):
+                copy(level, k, c).wait_send()
+
+
+ANY = pl.BlockSpec(memory_space=pl.ANY)
+VM = pl.BlockSpec(memory_space=pltpu.VMEM)
+
+
+def gather_first(n_ex, n_dp, og, info, pre):
+    dma = pltpu.SemaphoreType.DMA
+    lines, bits = n_ex // 2, n_dp.bit_length() - 1
+    return pl.pallas_call(
+        functools.partial(first_kernel, n_ex, n_dp),
+        out_shape=(
+            jax.ShapeDtypeStruct((n_ex,) + og.shape, og.dtype),
+            jax.ShapeDtypeStruct((n_ex,) + info.shape, info.dtype),
+            jax.ShapeDtypeStruct((n_dp,) + pre.shape, pre.dtype),
+        ),
+        in_specs=[ANY] * 3,
+        out_specs=[ANY] * 3,
+        scratch_shapes=[
+            dma((2, 2, 4, lines)),
+            dma((2,)),
+            dma((2, bits, n_dp // 2, 2)),
+            dma,
+        ],
+        compiler_params=pltpu.CompilerParams(
+            collective_id=0, has_side_effects=True, vmem_limit_bytes=48 << 20
+        ),
+    )(og, info, pre)
+
+
+def gather_second(n_ex, n_dp, tk, part):
+    dma = pltpu.SemaphoreType.DMA
+    lines, bits = n_ex // 2, n_dp.bit_length() - 1
+    rows, cols = part.shape[1:]
+    chunks = 4
+    half = [pltpu.VMEM((n_dp >> (b + 1), rows, cols), BF) for b in range(bits)]
+    return pl.pallas_call(
+        functools.partial(second_kernel, n_ex, n_dp, chunks),
+        out_shape=(
+            jax.ShapeDtypeStruct((n_ex,) + tk.shape, tk.dtype),
+            jax.ShapeDtypeStruct((rows, cols), F32),
+            jax.ShapeDtypeStruct((n_dp, rows, cols), BF),
+        ),
+        in_specs=[ANY, VM],
+        out_specs=[ANY, VM, VM],
+        scratch_shapes=[
+            dma((2, 1, 4, lines)),
+            dma((1,)),
+            dma((2, bits, n_dp // 2, chunks)),
+            dma((bits, 2, n_dp // 2, chunks)),
+        ]
+        + half
+        + half,
+        compiler_params=pltpu.CompilerParams(
+            collective_id=1, has_side_effects=True, vmem_limit_bytes=48 << 20
+        ),
+    )(tk, part)
 
 
 def body(tokens, out_grad, probs, expert_ids, dropped, preacts, w_gu, w_down):
@@ -50,21 +366,18 @@
 
     code = (expert_ids + EXPERTS * dropped).astype(F32)
     info = jnp.concatenate([code.T, probs.astype(F32).T], axis=0)
-    info = lax.all_gather(info, ("dp", "expert"), axis=0, tiled=False)
-    info = info.reshape(n_dp, n_ex, 2 * top, rows)
+    info = gather_rel(info, "dp")
 
     def spread(x):
         pieces = [
             lax.dynamic_slice_in_dim(x, (me ^ r) * part, part, axis=1) for r in range(n_dp)
         ]
-        got = jnp.stack(swap_rel(pieces, "dp"), axis=0)
-        return lax.all_gather(got, "expert", axis=0, tiled=False)
+        return jnp.stack(swap_rel(pieces, "dp"), axis=0)
 
     og = spread(out_grad)
     tk = spread(tokens)
-    pre = gather_rel(preacts[0], "dp").reshape(n_dp, local, n_ex, CAP, 2 * fw)
-
-    info = jnp.stack([info[me ^ r] for r in range(n_dp)], axis=1)
+    og, info, pre = gather_first(n_ex, n_dp, og, info, preacts.reshape(-1, 2 * fw))
+    pre = pre.reshape(n_dp, local, n_ex, CAP, 2 * fw)
     code_all, prob_all = info[:, :, :top], info[:, :, top:]
     experts = (mine * local + jnp.arange(local)).astype(F32)[:, None, None]
     kept_k = (code_all[:, :, None] == experts).astype(F32)
@@ -84,8 +397,10 @@
 
     gs = jnp.einsum("jreqt,jrtd->erjqd", pick, og, preferred_element_type=F32).astype(BF)
     proj = jnp.einsum("erjqd,efd->rejqf", gs, w_down, preferred_element_type=F32)
-    own = scatter_rel(proj, "dp", BF)
-    proj = gather_rel(own.astype(BF), "dp").astype(F32)
+    proj = proj.astype(BF).reshape(n_dp, -1, fw)
+    tk, own, proj = gather_second(n_ex, n_dp, tk, proj)
+    own = own.reshape(local, n_ex, CAP, fw)
+    proj = proj.reshape((n_dp,) + own.shape).astype(F32)
 
     gate, up = pre[..., :fw].astype(F32), pre[..., fw:].astype(F32)
     sig = jax.nn.sigmoid(gate)

time: 407 us -> 331 us (0.81)
  Pallas kernels: 0 us -> 113 us
  waiting for transfers between devices: 157 us -> 64.8 us
  blocking collectives: 113 us -> 40.3 us
  other arithmetic: 37.9 us -> 20.8 us
  matrix products: 47.6 us -> 42.7 us
    pallas_call x0 -> x2, Pallas kernels: none -> 113 us  [the longest x1 56.8 us: gather_second(): pl.pallas_call(functools.partial(second_kernel, n_ex, n_dp, chunks), out_...]
    ppermute x15 -> x11, waiting for transfers between devices: 89.4 us -> 3.41 us  [xor_permute(): return lax.ppermute(x, axis, [(a, a ^ bit) for a in range(n)])]
    all_gather x1 -> x0, blocking collectives: 72.8 us -> none  [body(): info = lax.all_gather(info, ('dp', 'expert'), axis=0, tiled=False)]
    convert_element_type x3 -> x0, other arithmetic: 15.2 us -> none  [the longest x1 7.74 us: body(): hidden_p = (ps * hidden).astype(BF)]
    another operation x3, other arithmetic: 11.1 us -> 0.01 us  [gather_rel(): buf = jnp.stack([buf, other], axis=1).reshape((-1,) + x.shape)]
    another operation x3, other arithmetic: 1.74 us -> 12.3 us  [the longest x2 1.72 us: spread(): got = jnp.stack(swap_rel(pieces, 'dp'), axis=0)]
    dot_general x1 -> x0, matrix products: 7.57 us -> none  [body(): jnp.einsum('rejqf,edf->erjqd', dgu, w_gu, preferred_element_type=F32)]
    another operation x1, local copies, waits for them, and re-layouts: 7.1 us -> 0.01 us  [gather_rel(): buf = jnp.stack([buf, other], axis=1).reshape((-1,) + x.shape)]
  transfers between devices with their start and end apart: 19 -> 13, of which waited for: 11 -> 3; matrix products, arithmetic and copies ran while one was open for 22% -> 16% of each run, Pallas kernels for 0% -> 17%
where the time goes in v2:
time: 331 us; the launch traced here: 330 us
  Pallas kernels  113 us (34%)
  waiting for transfers between devices  64.8 us (20%)
  matrix products  42.7 us (13%)
  blocking collectives  40.3 us (12%)
  other arithmetic  20.8 us (6%)
  between operations  17.4 us (5%)
  local copies, waits for them, and re-layouts  15.7 us (5%)
  starting transfers between devices  15 us (5%)
    reduce_scatter x1, waiting for transfers between devices, body(): tok = lax.psum_scatter(tok, 'expert', scatter_dimension=0, tiled=False)  61.4 us
    pallas_call x1, Pallas kernels, gather_second(): pl.pallas_call(functools.partial(second_kernel, n_ex, n_dp, chunks), out_...  56.8 us
    pallas_call x1, Pallas kernels, gather_first(): pl.pallas_call(functools.partial(first_kernel, n_ex, n_dp), out_shape=(ja...  56.4 us
    psum x1, blocking collectives, body(): lax.psum(square, ('dp', 'expert')) / (EXPERTS * 3 * width * fw)  40.3 us
    dot_general x1, matrix products, body(): jnp.einsum('erjqd,rejqf->edf', xs, dgu, preferred_element_type=F32)  10.9 us
    another operation x1, other arithmetic  10.1 us
    dot_general x1, matrix products, body(): jnp.einsum('jreqt,erjqd->jrtd', pick, slot_grad, preferred_element_type=F32)  9.18 us
    dot_general x1, matrix products, body(): jnp.einsum('rejqf,erjqd->efd', hidden_p, gs, preferred_element_type=F32)  9.13 us
  transfers between devices with their start and end apart: 13, of which 3 were waited for; matrix products, arithmetic and copies ran while one was open for 16% of the time, Pallas kernels for 17%

profile of v2, /device:TPU:0, one launch (start us, length us, event | category | flops | bytes accessed | tf_op | source)
XLA Modules:
  0.0 329.9 jit_solution(15633107975165189724)
XLA Ops:
  7.3 2.0 dynamic-slice_bitcast_fusion.5
  9.7 2.5 collective-permute-start.1
  13.8 1.7 collective-permute-start.3
  15.5 1.9 dynamic-slice_bitcast_fusion.4
  17.4 2.2 collective-permute-done.3
  19.6 1.2 collective-permute-done.4
  20.8 1.7 collective-permute-start.6
  22.6 1.1 pad_maximum_fusion.1.og
  23.8 1.5 copy-done.2
  25.3 56.4 %shard_map.119 = (bf16[8,4,128,512]{3,2,1,0:T(8,128)(2,1)}, f32[8,4,16,128]{3,2,1,0:T(8,128)S(1)}, bf16[4,1280,768]{2,1,0:T(8,128)(2,1)}) custom-call(bf16[4,128,512]{2,1,0:T(8,128)(2,1)S(1)} %pad_maximum_fusion.1.og, f32[4,16,128]{2,1,0:T(8,128)S(1)} %bitcast.111, bf16[1280,768]{1,0:T(8,128)(2,1)S(1)} %bitcast.109), custom_call_target="tpu_custom_call" | custom-call | tf_op jit(solution)/shard_map/pallas_call | solution.py:308
  82.6 4.0 %fusion.58 = (bf16[4,4,8,40,384]{4,3,2,1,0:T(8,128)(2,1)S(1)}, bf16[4,4,8,40,384]{4,3,2,1,0:T(8,128)(2,1)S(1)}) fusion(bf16[4,4,8,40,768]{4,3,2,1,0:T(8,128)(2,1)} %bitcast.113), kind=kLoop, calls=%fused_computation.98 | loop fusion | bytes 15728640 | tf_op jit(solution)/shard_map/slice | solution.py:405
  87.1 1.5 convert_bitcast_fusion.1
  88.6 5.7 %convert_bitcast_fusion.2 = bf16[4,4,8,40,384]{4,3,2,0,1:T(8,128)(2,1)S(1)} fusion(bf16[4,4,8,40,512]{4,3,0,2,1:T(8,128)(2,1)S(1)} %convert_bitcast_fusion.1, bf16[4,384,512]{2,1,0:T(8,128)(2,1)} %param.15), kind=kOutput, calls=%fused_computation.33 | convolution fusion | flops 2015232000 | bytes 10747904 | tf_op jit(solution)/shard_map/erjqd,efd->rejqf/dot_general | solution.py:399
  94.3 2.4 copy.42
  96.6 0.8 select_reduce_fusion
  97.5 1.1 pad_maximum_fusion.2.tk
  98.6 56.8 %shard_map.120 = (bf16[8,4,128,512]{3,2,1,0:T(8,128)(2,1)}, f32[1280,384]{1,0:T(8,128)S(1)}, bf16[4,1280,384]{2,1,0:T(8,128)(2,1)}) custom-call(bf16[4,128,512]{2,1,0:T(8,128)(2,1)S(1)} %pad_maximum_fusion.2.tk, bf16[4,1280,384]{2,1,0:T(8,128)(2,1)} %bitcast.112), custom_call_target="tpu_custom_call" | custom-call | tf_op jit(solution)/shard_map/pallas_call | solution.py:335
  155.4 10.1 %fusion.2 = (bf16[4,4,8,40,384]{4,3,1,0,2:T(8,128)(2,1)}, bf16[4,4,8,40,384]{4,3,1,0,2:T(8,128)(2,1)}, f32[4,4,8,40,384]{4,3,1,0,2:T(8,128)}) fusion(f32[4,4,8,40]{3,1,0,2:T(4,128)S(1)} %bitcast.115, bf16[4,4,8,40,384]{4,3,2,1,0:T(8,128)(2,1)S(1)} %get-tuple-element.24, bf16[4,4,8,40,384]{4,3,2,1,0:T(8,128)(2,1)S(1)} %get-tuple-element.23, ...), kind=kLoop, calls=%fused_computation.8 | loop fusion | flops 35389440 | bytes 27545600 | tf_op jit(solution)/shard_map/convert.3
  165.5 9.2 %bitcast_convert_fusion = bf16[8,4,128,512]{3,2,1,0:T(8,128)(2,1)} fusion(bf16[4,512,768]{2,1,0:T(8,128)(2,1)S(1)} %copy-done, f32[8,4,4,128]{3,2,1,0:T(4,128)S(1)} %copy.38, bf16[4,4,8,40,384]{4,3,1,0,2:T(8,128)(2,1)} %get-tuple-element.21, bf16[4,4,8,40,384]{4,3,1,0,2:T(8,128)(2,1)} %get-tuple-element.20), kind=kOutput, calls=%fused_computation.5 | convolution fusion | flops 4718723072 | bytes 15269888 | tf_op jit(solution)/shard_map/jreqt,erjqd->jrtd/dot_general | solution.py:417
  174.7 1.5 copy-done.4
  176.2 1.8 fusion.43
  178.5 0.9 select_reduce_fusion.1
  179.3 6.4 %all-to-all-start = ((f32[8,4,128]{2,1,0:T(4,128)}), f32[8,4,128]{2,1,0:T(4,128)S(1)}, u32[]{:S(2)}, u32[]{:S(2)}) async-start(f32[8,4,128]{2,1,0:T(4,128)} %select_reduce_fusion.1), calls=%async_computation.1 | async-start | bytes 32768 | tf_op jit(solution)/shard_map/all_to_all | solution.py:426
  185.8 6.2 %convert_bitcast_fusion = bf16[4,4,8,40,512]{4,3,1,2,0:T(8,128)(2,1)} fusion(bf16[8,4,128,512]{3,2,1,0:T(8,128)(2,1)} %get-tuple-element.16, f32[8,4,4,128]{3,2,1,0:T(4,128)S(1)} %copy.38), kind=kOutput, calls=%fused_computation.25 | convolution fusion | flops 674365440 | bytes 9502720 | tf_op jit(solution)/shard_map/jreqt,jrtd->erjqd/dot_general | solution.py:431
  191.9 10.9 %multiply_reduce_fusion = (f32[]{:T(128)}, f32[4,512,768]{2,1,0:T(8,128)}) fusion(bf16[4,4,8,40,512]{4,3,1,2,0:T(8,128)(2,1)} %convert_bitcast_fusion, bf16[4,4,8,40,384]{4,3,1,0,2:T(8,128)(2,1)} %get-tuple-element.21, bf16[4,4,8,40,384]{4,3,1,0,2:T(8,128)(2,1)S(1)} %copy-done.9), kind=kOutput, calls=%fused_computation.19 | convolution fusion | flops 4045406208 | bytes 19398660 | tf_op jit(solution)/shard_map/erjqd,rejqf->edf/dot_general | solution.py:433
  202.8 61.4 %reduce-scatter.2.cloned.1.call-done = bf16[1,4,128,512]{3,2,1,0:T(8,128)(2,1)} async-done(((bf16[8,4,128,512]{3,2,1,0:T(8,128)(2,1)}), bf16[1,4,128,512]{3,2,1,0:T(8,128)(2,1)}) %reduce-scatter.2.cloned.1.call-update) | async-done | bytes 524304 | tf_op jit(solution)/shard_map/reduce_scatter | solution.py:418
  264.2 1.8 slice_bitcast_fusion.5
  266.0 1.5 collective-permute-start.9
  267.9 9.1 %multiply_reduce_fusion.1 = (f32[]{:T(128)}, f32[4,384,512]{2,1,0:T(8,128)}) fusion(bf16[4,4,8,40,512]{4,3,0,2,1:T(8,128)(2,1)} %copy-done.7, f32[4,4,8,40]{3,1,0,2:T(4,128)S(1)} %bitcast.116, bf16[4,4,8,40,384]{4,3,2,1,0:T(8,128)(2,1)} %copy-done.5, bf16[4,4,8,40,384]{4,3,2,1,0:T(8,128)(2,1)} %copy-done.6), kind=kOutput, calls=%fused_computation.37 | convolution fusion | flops 2032533504 | bytes 16273412 | tf_op jit(solution)/shard_map/rejqf,erjqd->efd/dot_general | solution.py:432
  278.3 40.3 %psum.7 = f32[]{:T(128)} all-reduce(f32[]{:T(128)S(6)} %add.87), channel_id=1, replica_groups=mesh['dp'=4,'expert'=8] {'dp','expert'}, use_global_device_ids=true, to_apply=%region_10.11 | all-reduce | flops 1 | bytes 8 | tf_op jit(solution)/shard_map/psum | solution.py:435
  319.9 1.1 pad_maximum_fusion.3
  321.1 0.8 pad_maximum_fusion.4
  (55 shorter events, 4.9 us)
Async XLA Ops:
  7.2 158.3 %copy-start = (bf16[4,512,768]{2,1,0:T(8,128)(2,1)S(1)}, bf16[4,512,768]{2,1,0:T(8,128)(2,1)}, u32[]{:S(2)}) copy-start(bf16[4,512,768]{2,1,0:T(8,128)(2,1)} %param.14) | copy-start | bytes 9437188
  7.2 257.0 %reduce-scatter.2.cloned.1.call-start = ((), (), s32[]{:S(2)}) async-start(), calls=%async_computation.2 | async-start | bytes 4718592 | tf_op jit(solution)/shard_map/reduce_scatter | solution.py:418
  9.3 13.3 %collective-permute-start = (bf16[128,512]{1,0:T(8,128)(2,1)}, bf16[128,512]{1,0:T(8,128)(2,1)}, u32[]{:S(2)}, u32[]{:S(2)}) collective-permute-start(bf16[128,512]{1,0:T(8,128)(2,1)} %get-tuple-element.38), channel_id=1, source_target_pairs={{0,8},{8,0},{16,24},{24,16},{1,9},{9,1},{17,25},{25,17},{2,10},{10... | collective-permute-start | bytes 393224 | tf_op jit(solution)/shard_map/ppermute | solution.py:18
  9.7 12.9 %collective-permute-start.1 = (bf16[128,512]{1,0:T(8,128)(2,1)}, bf16[128,512]{1,0:T(8,128)(2,1)}, u32[]{:S(2)}, u32[]{:S(2)}) collective-permute-start(bf16[128,512]{1,0:T(8,128)(2,1)} %get-tuple-element.40), channel_id=1, source_target_pairs={{0,16},{8,24},{16,0},{24,8},{1,17},{9,25},{17,1},{25,9},{2,18},{10... | collective-permute-start | bytes 393224 | tf_op jit(solution)/shard_map/ppermute | solution.py:18
  12.2 10.4 %collective-permute-start.2 = (bf16[128,512]{1,0:T(8,128)(2,1)}, bf16[128,512]{1,0:T(8,128)(2,1)}, u32[]{:S(2)}, u32[]{:S(2)}) collective-permute-start(bf16[128,512]{1,0:T(8,128)(2,1)} %get-tuple-element.39), channel_id=1, source_target_pairs={{0,24},{8,16},{16,8},{24,0},{1,25},{9,17},{17,9},{25,1},{2,26},{10... | collective-permute-start | bytes 393224 | tf_op jit(solution)/shard_map/ppermute | solution.py:18
  13.8 5.8 %collective-permute-start.3 = (f32[1,16,128]{2,1,0:T(8,128)S(1)}, f32[1,16,128]{2,1,0:T(8,128)S(1)}, u32[]{:S(2)}, u32[]{:S(2)}) collective-permute-start(f32[1,16,128]{2,1,0:T(8,128)S(1)} %get-tuple-element.46), channel_id=1, source_target_pairs={{0,16},{8,24},{16,0},{24,8},{1,17},{9,25},{17,1},{25,9},{2,18},{10... | collective-permute-start | bytes 24584 | tf_op jit(solution)/shard_map/ppermute | solution.py:18
  17.4 80.1 %collective-permute-start.5 = (bf16[128,512]{1,0:T(8,128)(2,1)}, bf16[128,512]{1,0:T(8,128)(2,1)}, u32[]{:S(2)}, u32[]{:S(2)}) collective-permute-start(bf16[128,512]{1,0:T(8,128)(2,1)} %get-tuple-element.34), channel_id=1, source_target_pairs={{0,8},{8,0},{16,24},{24,16},{1,9},{9,1},{17,25},{25,17},{2,10},{10... | collective-permute-start | bytes 393224 | tf_op jit(solution)/shard_map/ppermute | solution.py:18
  19.6 1.2 collective-permute-start.4
  20.8 76.7 %collective-permute-start.6 = (bf16[128,512]{1,0:T(8,128)(2,1)}, bf16[128,512]{1,0:T(8,128)(2,1)}, u32[]{:S(2)}, u32[]{:S(2)}) collective-permute-start(bf16[128,512]{1,0:T(8,128)(2,1)} %get-tuple-element.36), channel_id=1, source_target_pairs={{0,16},{8,24},{16,0},{24,8},{1,17},{9,25},{17,1},{25,9},{2,18},{10... | collective-permute-start | bytes 393224 | tf_op jit(solution)/shard_map/ppermute | solution.py:18
  22.5 74.9 %collective-permute-start.7 = (bf16[128,512]{1,0:T(8,128)(2,1)}, bf16[128,512]{1,0:T(8,128)(2,1)}, u32[]{:S(2)}, u32[]{:S(2)}) collective-permute-start(bf16[128,512]{1,0:T(8,128)(2,1)} %get-tuple-element.35), channel_id=1, source_target_pairs={{0,24},{8,16},{16,8},{24,0},{1,25},{9,17},{17,9},{25,1},{2,26},{10... | collective-permute-start | bytes 393224 | tf_op jit(solution)/shard_map/ppermute | solution.py:18
  23.7 1.5 copy-start.2
  82.6 4.5 %copy-start.8 = (bf16[8,4,128,512]{3,2,1,0:T(8,128)(2,1)S(1)}, bf16[8,4,128,512]{3,2,1,0:T(8,128)(2,1)}, u32[]{:S(2)}) copy-start(bf16[8,4,128,512]{3,2,1,0:T(8,128)(2,1)} %get-tuple-element.12) | copy-start | bytes 12582916
  86.6 68.8 %copy-start.5 = (bf16[4,4,8,40,384]{4,3,2,1,0:T(8,128)(2,1)}, bf16[4,4,8,40,384]{4,3,2,1,0:T(8,128)(2,1)S(1)}, u32[]{:S(2)}) copy-start(bf16[4,4,8,40,384]{4,3,2,1,0:T(8,128)(2,1)S(1)} %get-tuple-element.23) | copy-start | bytes 11796484
  86.6 68.8 %copy-start.6 = (bf16[4,4,8,40,384]{4,3,2,1,0:T(8,128)(2,1)}, bf16[4,4,8,40,384]{4,3,2,1,0:T(8,128)(2,1)S(1)}, u32[]{:S(2)}) copy-start(bf16[4,4,8,40,384]{4,3,2,1,0:T(8,128)(2,1)S(1)} %get-tuple-element.24) | copy-start | bytes 11796484
  88.6 5.7 %copy-start.7 = (bf16[4,4,8,40,512]{4,3,0,2,1:T(8,128)(2,1)}, bf16[4,4,8,40,512]{4,3,0,2,1:T(8,128)(2,1)S(1)}, u32[]{:S(2)}) copy-start(bf16[4,4,8,40,512]{4,3,0,2,1:T(8,128)(2,1)S(1)} %convert_bitcast_fusion.1) | copy-start | bytes 15728644
  155.4 10.1 %copy-start.3 = (f32[1280,384]{1,0:T(8,128)}, f32[1280,384]{1,0:T(8,128)S(1)}, u32[]{:S(2)}) copy-start(f32[1280,384]{1,0:T(8,128)S(1)} %get-tuple-element.15) | copy-start | bytes 5898244
  174.7 1.5 copy-start.4
  179.3 140.0 %all-to-all-start = ((f32[8,4,128]{2,1,0:T(4,128)}), f32[8,4,128]{2,1,0:T(4,128)S(1)}, u32[]{:S(2)}, u32[]{:S(2)}) async-start(f32[8,4,128]{2,1,0:T(4,128)} %select_reduce_fusion.1), calls=%async_computation.1 | async-start | bytes 32768 | tf_op jit(solution)/shard_map/all_to_all | solution.py:426
  185.8 6.2 %copy-start.9 = (bf16[4,4,8,40,384]{4,3,1,0,2:T(8,128)(2,1)S(1)}, bf16[4,4,8,40,384]{4,3,1,0,2:T(8,128)(2,1)}, u32[]{:S(2)}) copy-start(bf16[4,4,8,40,384]{4,3,1,0,2:T(8,128)(2,1)} %get-tuple-element.20) | copy-start | bytes 11796484
  266.0 53.9 %collective-permute-start.8 = (bf16[128,512]{1,0:T(8,128)(2,1)}, bf16[128,512]{1,0:T(8,128)(2,1)}, u32[]{:S(2)}, u32[]{:S(2)}) collective-permute-start(bf16[128,512]{1,0:T(8,128)(2,1)} %get-tuple-element.32), channel_id=1, source_target_pairs={{0,8},{8,0},{16,24},{24,16},{1,9},{9,1},{17,25},{25,17},{2,10},{10... | collective-permute-start | bytes 393224 | tf_op jit(solution)/shard_map/ppermute | solution.py:18
  266.0 53.9 %collective-permute-start.9 = (bf16[128,512]{1,0:T(8,128)(2,1)}, bf16[128,512]{1,0:T(8,128)(2,1)}, u32[]{:S(2)}, u32[]{:S(2)}) collective-permute-start(bf16[128,512]{1,0:T(8,128)(2,1)} %get-tuple-element.31), channel_id=1, source_target_pairs={{0,16},{8,24},{16,0},{24,8},{1,17},{9,25},{17,1},{25,9},{2,18},{10... | collective-permute-start | bytes 393224 | tf_op jit(solution)/shard_map/ppermute | solution.py:18
  267.5 52.4 %collective-permute-start.10 = (bf16[128,512]{1,0:T(8,128)(2,1)S(1)}, bf16[128,512]{1,0:T(8,128)(2,1)}, u32[]{:S(2)}, u32[]{:S(2)}) collective-permute-start(bf16[128,512]{1,0:T(8,128)(2,1)S(1)} %get-tuple-element.30), channel_id=1, source_target_pairs={{0,24},{8,16},{16,8},{24,0},{1,25},{9,17},{17,9},{25,1},{2,26},{10... | collective-permute-start | bytes 393224 | tf_op jit(solution)/shard_map/ppermute | solution.py:18
  267.9 54.0 %copy-start.1 = (bf16[4,512,768]{2,1,0:T(8,128)(2,1)S(1)}, bf16[4,512,768]{2,1,0:T(8,128)(2,1)}, u32[]{:S(2)}) copy-start(bf16[4,512,768]{2,1,0:T(8,128)(2,1)} %param.14) | copy-start | bytes 9437188
Sparse Core Ops, SparseCore 0:
  174.8 89.3 reduce-scatter.1

commit v3 on v2

--- a/solution.py
+++ b/solution.py
@@ -355,6 +355,175 @@
     )(tk, part)
 
 
+def mixed(me, r):
+    bit = 1
+    while bit <= r:
+        if r & bit:
+            me = flip(me, bit)
+        bit *= 2
+    return me
+
+
+def third_kernel(n_ex, n_dp, tok, square, out, total_out, got, below, above, fin, box, tile, x_sems, line_sems, dp_sems, sum_sems, all_sems):
+    j, me = lax.axis_index("expert"), lax.axis_index("dp")
+    lines = n_ex // 2
+    z, x = j // 2, j % 2
+    partner = z * 2 + 1 - x
+    barrier = pltpu.get_barrier_semaphore()
+    for k in range(1, n_ex):
+        pl.semaphore_signal(
+            barrier, inc=1, device_id={"expert": (j + k) % n_ex}, device_id_type=pl.DeviceIdType.MESH
+        )
+    for r in range(1, n_dp):
+        pl.semaphore_signal(
+            barrier, inc=1, device_id={"dp": mixed(me, r)}, device_id_type=pl.DeviceIdType.MESH
+        )
+    pl.semaphore_wait(barrier, n_ex - 1 + n_dp - 1)
+
+    def pair(side, d):
+        there = z + d if side == 0 else z - d
+        return remote(tok.at[there * 2 + 1 - x], got.at[there], x_sems, (side, d), "expert", partner)
+
+    def on_line(side, d):
+        return z + d < lines if side == 0 else z - d >= 0
+
+    for d in range(lines - 1, 0, -1):
+        for side in (0, 1):
+
+            @pl.when(on_line(side, d))
+            def _():
+                pair(side, d).start()
+
+    pair(0, 0).start()
+
+    levels = n_dp.bit_length() - 1
+
+    def swap_sum(level):
+        return remote(tile.at[level], box.at[n_ex + level], sum_sems, (level,), "dp", flip(me, 1 << level))
+
+    def hand(k):
+        return remote(tile.at[levels], box.at[j], all_sems, (k,), "expert", (j + k) % n_ex)
+
+    def handed(k):
+        return remote(tile.at[levels], box.at[(j - k + n_ex) % n_ex], all_sems, (k,), "expert", (j + k) % n_ex)
+
+    tile[0] = square[...]
+    for level in range(levels):
+        swap_sum(level).start()
+        swap_sum(level).wait()
+        tile[level + 1] = tile[level] + box[n_ex + level]
+    for k in range(1, n_ex):
+        hand(k).start()
+    box[j] = tile[levels]
+
+    def pass_on(side, d):
+        there = z + d if side == 0 else z - d
+        dst = below if side == 0 else above
+        return remote(
+            got.at[there], dst.at[d - 1], line_sems, (side, d - 1), "expert", j + 2 if side == 0 else j - 2
+        )
+
+    def arrived(side, d):
+        dst = below if side == 0 else above
+        return remote(tok.at[0], dst.at[d], line_sems, (side, d), "expert", partner)
+
+    def landed(side, d):
+        there = z + d if side == 0 else z - d
+        return remote(tok.at[0], got.at[there], x_sems, (side, d), "expert", partner)
+
+    for d in range(lines - 1, 0, -1):
+        for side in (0, 1):
+
+            @pl.when(on_line(side, d))
+            def _():
+                there = z + d if side == 0 else z - d
+                landed(side, d).wait_recv()
+                got[there] = (tok[there * 2 + x].astype(F32) + got[there].astype(F32)).astype(BF)
+                if d <= lines - 2:
+
+                    @pl.when((z > 0) if side == 0 else (z < lines - 1))
+                    def _():
+                        arrived(side, d).wait_recv()
+                        more = below[d] if side == 0 else above[d]
+                        got[there] = (got[there].astype(F32) + more.astype(F32)).astype(BF)
+
+                pass_on(side, d).start()
+
+    landed(0, 0).wait_recv()
+    fin[...] = tok[j].astype(F32) + got[z].astype(F32)
+
+    @pl.when(z > 0)
+    def _():
+        arrived(0, 0).wait_recv()
+        fin[...] += below[0].astype(F32)
+
+    @pl.when(z < lines - 1)
+    def _():
+        arrived(1, 0).wait_recv()
+        fin[...] += above[0].astype(F32)
+
+    got[z] = fin[...].astype(BF)
+
+    def slice_to(r):
+        return remote(got.at[z, r], out.at[me], dp_sems, (r,), "dp", mixed(me, r))
+
+    def slice_from(r):
+        return remote(got.at[z, r], out.at[mixed(me, r)], dp_sems, (r,), "dp", mixed(me, r))
+
+    for r in range(n_dp - 1, 0, -1):
+        slice_to(r).start()
+    out[me] = got[z, 0]
+    for k in range(1, n_ex):
+        handed(k).wait_recv()
+        hand(k).wait_send()
+    total = box[0]
+    for k in range(1, n_ex):
+        total = total + box[k]
+    total_out[...] = total
+    for r in range(1, n_dp):
+        slice_from(r).wait_recv()
+        slice_to(r).wait_send()
+    pair(0, 0).wait_send()
+    for d in range(1, lines):
+        for side in (0, 1):
+
+            @pl.when(on_line(side, d))
+            def _():
+                pair(side, d).wait_send()
+                pass_on(side, d).wait_send()
+
+
+def scatter_third(n_ex, n_dp, tok, square):
+    dma = pltpu.SemaphoreType.DMA
+    lines, bits = n_ex // 2, n_dp.bit_length() - 1
+    block = tok.shape[1:]
+    return pl.pallas_call(
+        functools.partial(third_kernel, n_ex, n_dp),
+        out_shape=(
+            jax.ShapeDtypeStruct(block, BF),
+            jax.ShapeDtypeStruct(square.shape, F32),
+        ),
+        in_specs=[VM] * 2,
+        out_specs=[VM] * 2,
+        scratch_shapes=[
+            pltpu.VMEM((lines,) + block, BF),
+            pltpu.VMEM((lines - 1,) + block, BF),
+            pltpu.VMEM((lines - 1,) + block, BF),
+            pltpu.VMEM(block, F32),
+            pltpu.VMEM((n_ex + bits,) + square.shape, F32),
+            pltpu.VMEM((bits + 1,) + square.shape, F32),
+            dma((2, 2, lines)),
+            dma((2, 2, lines)),
+            dma((2, n_dp)),
+            dma((2, bits)),
+            dma((2, n_ex)),
+        ],
+        compiler_params=pltpu.CompilerParams(
+            collective_id=2, has_side_effects=True, vmem_limit_bytes=56 << 20
+        ),
+    )(tok, square)
+
+
 def body(tokens, out_grad, probs, expert_ids, dropped, preacts, w_gu, w_down):
     n_dp, n_ex = lax.axis_size("dp"), lax.axis_size("expert")
     local = EXPERTS // n_ex
@@ -415,11 +584,6 @@
 
     slot_grad = jnp.einsum("rejqf,edf->erjqd", dgu, w_gu, preferred_element_type=F32).astype(BF)
     tok = jnp.einsum("jreqt,erjqd->jrtd", pick, slot_grad, preferred_element_type=F32).astype(BF)
-    tok = lax.psum_scatter(tok, "expert", scatter_dimension=0, tiled=False)
-    tok = swap_rel([tok[r] for r in range(n_dp)], "dp")
-    tok = jnp.stack(tok, axis=0)
-    tok_grad = jnp.concatenate([tok[me ^ p] for p in range(n_dp)], axis=-1)
-
     back = jnp.sum(
         jnp.where(hot[:, 0], jnp.transpose(slot_prob, (1, 0, 2))[..., None], 0.0), axis=2
     )
@@ -432,7 +596,9 @@
     grad_down = jnp.einsum("rejqf,erjqd->efd", hidden_p, gs, preferred_element_type=F32)
     grad_gu = jnp.einsum("erjqd,rejqf->edf", xs, dgu, preferred_element_type=F32)
     square = jnp.sum(grad_gu * grad_gu) + jnp.sum(grad_down * grad_down)
-    mean_square = lax.psum(square, ("dp", "expert")) / (EXPERTS * 3 * width * fw)
+    tok, total = scatter_third(n_ex, n_dp, tok, jnp.full((8, 128), square, F32))
+    tok_grad = jnp.transpose(tok, (1, 0, 2)).reshape(rows, width)
+    mean_square = total[0, 0] / (EXPERTS * 3 * width * fw)
     return tok_grad, prob_grad, grad_gu, grad_down, mean_square
 
 

time: 331 us -> 269 us (0.81)
  Pallas kernels: 113 us -> 175 us
  waiting for transfers between devices: 64.8 us -> 5.23 us
  blocking collectives: 40.3 us -> 0 us
  between operations: 17.4 us -> 3.95 us
  other arithmetic: 20.8 us -> 14.7 us
  starting transfers between devices: 15 us -> 10.8 us
    pallas_call x0 -> x1, Pallas kernels: none -> 61.4 us  [scatter_third(): pl.pallas_call(functools.partial(third_kernel, n_ex, n_dp), out_shape=(ja...]
    reduce_scatter x1 -> x0, waiting for transfers between devices: 61.4 us -> none  [body(): tok = lax.psum_scatter(tok, 'expert', scatter_dimension=0, tiled=False)]
    psum x1 -> x0, blocking collectives: 40.3 us -> none  [body(): lax.psum(square, ('dp', 'expert')) / (EXPERTS * 3 * width * fw)]
    another operation x2 -> x1, other arithmetic: 11.2 us -> 7.33 us
    ppermute x11 -> x8, starting transfers between devices: 8.51 us -> 7.32 us  [xor_permute(): return lax.ppermute(x, axis, [(a, a ^ bit) for a in range(n)])]
  transfers between devices with their start and end apart: 13 -> 9, of which waited for: 3 -> 3; matrix products, arithmetic and copies ran while one was open for 16% -> 20% of each run, Pallas kernels for 17% -> 43%
where the time goes in v3:
time: 269 us
  Pallas kernels  175 us (65%)
  matrix products  43.9 us (16%)
  local copies, waits for them, and re-layouts  15.6 us (6%)
  other arithmetic  14.7 us (5%)
  starting transfers between devices  10.8 us (4%)
  waiting for transfers between devices  5.23 us (2%)
  between operations  3.95 us (1%)
    pallas_call x1, Pallas kernels, scatter_third(): pl.pallas_call(functools.partial(third_kernel, n_ex, n_dp), out_shape=(ja...  61.4 us
    pallas_call x1, Pallas kernels, gather_second(): pl.pallas_call(functools.partial(second_kernel, n_ex, n_dp, chunks), out_...  59.1 us
    pallas_call x1, Pallas kernels, gather_first(): pl.pallas_call(functools.partial(first_kernel, n_ex, n_dp), out_shape=(ja...  54 us
    dot_general x1, matrix products, body(): jnp.einsum('erjqd,rejqf->edf', xs, dgu, preferred_element_type=F32)  12.5 us
    dot_general x1, matrix products, body(): jnp.einsum('jreqt,erjqd->jrtd', pick, slot_grad, preferred_element_type=F32)  9.16 us
    dot_general x1, matrix products, body(): jnp.einsum('rejqf,erjqd->efd', hidden_p, gs, preferred_element_type=F32)  8.99 us
    another operation x1, other arithmetic  7.33 us
    ppermute x8, starting transfers between devices, xor_permute(): return lax.ppermute(x, axis, [(a, a ^ bit) for a in range(n)])  7.32 us
  transfers between devices with their start and end apart: 9, of which 3 were waited for; matrix products, arithmetic and copies ran while one was open for 20% of the time, Pallas kernels for 43%

profile of v3, /device:TPU:0, one launch (start us, length us, event | category | flops | bytes accessed | tf_op | source)
XLA Modules:
  0.0 268.7 jit_solution(3543986759369324617)
XLA Ops:
  0.6 0.8 convert_bitcast_fusion.4
  1.5 0.8 convert_bitcast_fusion.5
  2.3 3.0 %collective-permute-start.3 = (f32[1,16,128]{2,1,0:T(8,128)S(1)}, f32[1,16,128]{2,1,0:T(8,128)S(1)}, u32[]{:S(2)}, u32[]{:S(2)}) collective-permute-start(f32[1,16,128]{2,1,0:T(8,128)S(1)} %get-tuple-element.57), channel_id=1, source_target_pairs={{0,16},{8,24},{16,0},{24,8},{1,17},{9,25},{17,1},{25,9},{2,18},{10... | collective-permute-start | bytes 24584 | tf_op jit(solution)/shard_map/ppermute | solution.py:18
  5.3 1.9 dynamic-slice_bitcast_fusion
  7.2 1.8 dynamic-slice_bitcast_fusion.1
  9.5 1.6 collective-permute-start.1
  11.5 1.0 collective-permute-done.4
  12.6 1.7 collective-permute-start.6
  14.3 1.1 collective-permute-done.2
  15.4 3.2 %collective-permute-done.1 = bf16[128,512]{1,0:T(8,128)(2,1)} collective-permute-done((bf16[128,512]{1,0:T(8,128)(2,1)}, bf16[128,512]{1,0:T(8,128)(2,1)}, u32[]{:S(2)}, u32[]{:S(2)}) %collective-permute-start.1) | collective-permute-done | bytes 131104 | tf_op jit(solution)/shard_map/ppermute | solution.py:18
  18.6 1.1 pad_maximum_fusion.1.og
  19.7 1.5 copy-done.1
  21.3 54.0 %shard_map.119 = (bf16[8,4,128,512]{3,2,1,0:T(8,128)(2,1)}, f32[8,4,16,128]{3,2,1,0:T(8,128)S(1)}, bf16[4,1280,768]{2,1,0:T(8,128)(2,1)}) custom-call(bf16[4,128,512]{2,1,0:T(8,128)(2,1)S(1)} %pad_maximum_fusion.1.og, f32[4,16,128]{2,1,0:T(8,128)S(1)} %bitcast.95, bf16[1280,768]{1,0:T(8,128)(2,1)S(1)} %bitcast.93), custom_call_target="tpu_custom_call" | custom-call | tf_op jit(solution)/shard_map/pallas_call | solution.py:308
  76.6 3.8 %convert_bitcast_fusion.1 = bf16[4,4,8,40,512]{4,3,0,2,1:T(8,128)(2,1)S(1)} fusion(bf16[8,4,128,512]{3,2,1,0:T(8,128)(2,1)} %get-tuple-element.14, f32[8,4,4,128]{3,2,1,0:T(4,128)S(1)} %copy.57), kind=kOutput, calls=%fused_computation.28 | convolution fusion | flops 674365440 | bytes 9502720 | tf_op jit(solution)/shard_map/jreqt,jrtd->erjqd/dot_general | solution.py:567
  80.4 3.1 %convert_bitcast_fusion.2 = bf16[4,4,8,40,384]{4,3,2,0,1:T(8,128)(2,1)S(1)} fusion(bf16[4,4,8,40,512]{4,3,0,2,1:T(8,128)(2,1)S(1)} %convert_bitcast_fusion.1, bf16[4,384,512]{2,1,0:T(8,128)(2,1)S(1)} %copy-done.6), kind=kOutput, calls=%fused_computation.33 | convolution fusion | flops 2015232000 | bytes 10747904 | tf_op jit(solution)/shard_map/erjqd,efd->rejqf/dot_general | solution.py:568
  83.6 2.3 copy.61
  85.9 0.8 select_reduce_fusion
  86.7 1.0 pad_maximum_fusion.2.tk
  87.7 59.1 %shard_map.120 = (bf16[8,4,128,512]{3,2,1,0:T(8,128)(2,1)}, f32[1280,384]{1,0:T(8,128)S(1)}, bf16[4,1280,384]{2,1,0:T(8,128)(2,1)}) custom-call(bf16[4,128,512]{2,1,0:T(8,128)(2,1)S(1)} %pad_maximum_fusion.2.tk, bf16[4,1280,384]{2,1,0:T(8,128)(2,1)} %bitcast.96), custom_call_target="tpu_custom_call" | custom-call | tf_op jit(solution)/shard_map/pallas_call | solution.py:335
  146.8 6.1 %convert_bitcast_fusion = bf16[4,4,8,40,512]{4,3,1,2,0:T(8,128)(2,1)} fusion(bf16[8,4,128,512]{3,2,1,0:T(8,128)(2,1)} %get-tuple-element.17, f32[8,4,4,128]{3,2,1,0:T(4,128)S(1)} %copy.57), kind=kOutput, calls=%fused_computation.25 | convolution fusion | flops 674365440 | bytes 9502720 | tf_op jit(solution)/shard_map/jreqt,jrtd->erjqd/dot_general | solution.py:595
  153.0 1.2 fusion.58
  154.2 0.9 copy-done.5
  155.1 7.3 %fusion.2 = (bf16[4,4,8,40,384]{4,3,1,0,2:T(8,128)(2,1)}, bf16[4,4,8,40,384]{4,3,1,0,2:T(8,128)(2,1)}, f32[4,4,8,40,384]{4,3,1,0,2:T(8,128)S(1)}) fusion(f32[4,4,8,40]{3,1,0,2:T(4,128)S(1)} %bitcast.103, bf16[4,4,8,40,384]{4,3,2,1,0:T(8,128)(2,1)S(1)} %get-tuple-element.42, bf16[4,4,8,40,384]{4,3,2,1,0:T(8,128)(2,1)S(1)} %get-tuple-element.43, ...), kind=kLoop, calls=%fused_computation.8 | loop fusion | flops 35389440 | bytes 27545600 | tf_op jit(solution)/shard_map/convert.3
  162.8 0.9 select_reduce_fusion.1
  163.6 3.5 %all-to-all-start = ((f32[8,4,128]{2,1,0:T(4,128)}), f32[8,4,128]{2,1,0:T(4,128)S(1)}, u32[]{:S(2)}, u32[]{:S(2)}) async-start(f32[8,4,128]{2,1,0:T(4,128)} %select_reduce_fusion.1), calls=%async_computation | async-start | bytes 32768 | tf_op jit(solution)/shard_map/all_to_all | solution.py:590
  167.2 12.5 %multiply_reduce_fusion = (f32[]{:T(128)}, f32[4,512,768]{2,1,0:T(8,128)}) fusion(bf16[4,4,8,40,512]{4,3,1,2,0:T(8,128)(2,1)} %convert_bitcast_fusion, bf16[4,4,8,40,384]{4,3,1,0,2:T(8,128)(2,1)} %get-tuple-element.40, bf16[4,4,8,40,384]{4,3,1,0,2:T(8,128)(2,1)} %get-tuple-element.39), kind=kOutput, calls=%fused_computation.19 | convolution fusion | flops 4045406208 | bytes 19398660 | tf_op jit(solution)/shard_map/erjqd,rejqf->edf/dot_general | solution.py:597
  179.7 9.2 %bitcast_convert_fusion.tok = bf16[8,4,128,512]{3,2,1,0:T(8,128)(2,1)} fusion(bf16[4,512,768]{2,1,0:T(8,128)(2,1)S(1)} %copy-done, f32[8,4,4,128]{3,2,1,0:T(4,128)S(1)} %copy.57, bf16[4,4,8,40,384]{4,3,1,0,2:T(8,128)(2,1)} %get-tuple-element.40, bf16[4,4,8,40,384]{4,3,1,0,2:T(8,128)(2,1)} %get-tuple-element.39), kind=kOutput, calls=%fused_computation.5 | convolution fusion | flops 4718723072 | bytes 15269888 | tf_op jit(solution)/shard_map/jreqt,erjqd->jrtd/dot_general | solution.py:586
  188.8 9.0 %multiply_reduce_fusion.1 = (f32[]{:T(128)}, f32[4,384,512]{2,1,0:T(8,128)}) fusion(bf16[4,4,8,40,512]{4,3,0,2,1:T(8,128)(2,1)} %copy-done.4, f32[4,4,8,40]{3,1,0,2:T(4,128)S(1)} %bitcast.104, bf16[4,4,8,40,384]{4,3,2,1,0:T(8,128)(2,1)} %copy-done.2, bf16[4,4,8,40,384]{4,3,2,1,0:T(8,128)(2,1)} %copy-done.3), kind=kOutput, calls=%fused_computation.37 | convolution fusion | flops 2032533504 | bytes 16273412 | tf_op jit(solution)/shard_map/rejqf,erjqd->efd/dot_general | solution.py:596
  199.7 61.4 %shard_map.121 = (bf16[4,128,512]{2,1,0:T(8,128)(2,1)}, f32[8,128]{1,0:T(8,128)}) custom-call(bf16[8,4,128,512]{3,2,1,0:T(8,128)(2,1)} %bitcast_convert_fusion.tok, f32[8,128]{1,0:T(8,128)} %broadcast_in_dim.64.square), custom_call_target="tpu_custom_call" | custom-call | tf_op jit(solution)/shard_map/pallas_call | solution.py:500
  261.1 1.2 slice.27
  262.3 2.0 copy.69
  264.3 2.0 copy.73
  (45 shorter events, 3.9 us)
Async XLA Ops:
  0.6 179.0 %copy-start = (bf16[4,512,768]{2,1,0:T(8,128)(2,1)S(1)}, bf16[4,512,768]{2,1,0:T(8,128)(2,1)}, u32[]{:S(2)}) copy-start(bf16[4,512,768]{2,1,0:T(8,128)(2,1)} %param.14) | copy-start | bytes 9437188
  2.3 8.8 %collective-permute-start.3 = (f32[1,16,128]{2,1,0:T(8,128)S(1)}, f32[1,16,128]{2,1,0:T(8,128)S(1)}, u32[]{:S(2)}, u32[]{:S(2)}) collective-permute-start(f32[1,16,128]{2,1,0:T(8,128)S(1)} %get-tuple-element.57), channel_id=1, source_target_pairs={{0,16},{8,24},{16,0},{24,8},{1,17},{9,25},{17,1},{25,9},{2,18},{10... | collective-permute-start | bytes 24584 | tf_op jit(solution)/shard_map/ppermute | solution.py:18
  7.2 79.5 %collective-permute-start.5 = (bf16[128,512]{1,0:T(8,128)(2,1)}, bf16[128,512]{1,0:T(8,128)(2,1)}, u32[]{:S(2)}, u32[]{:S(2)}) collective-permute-start(bf16[128,512]{1,0:T(8,128)(2,1)} %get-tuple-element.45), channel_id=1, source_target_pairs={{0,8},{8,0},{16,24},{24,16},{1,9},{9,1},{17,25},{25,17},{2,10},{10... | collective-permute-start | bytes 393224 | tf_op jit(solution)/shard_map/ppermute | solution.py:18
  9.0 3.6 %collective-permute-start = (bf16[128,512]{1,0:T(8,128)(2,1)}, bf16[128,512]{1,0:T(8,128)(2,1)}, u32[]{:S(2)}, u32[]{:S(2)}) collective-permute-start(bf16[128,512]{1,0:T(8,128)(2,1)} %get-tuple-element.49), channel_id=1, source_target_pairs={{0,8},{8,0},{16,24},{24,16},{1,9},{9,1},{17,25},{25,17},{2,10},{10... | collective-permute-start | bytes 393224 | tf_op jit(solution)/shard_map/ppermute | solution.py:18
  9.5 5.9 %collective-permute-start.2 = (bf16[128,512]{1,0:T(8,128)(2,1)}, bf16[128,512]{1,0:T(8,128)(2,1)}, u32[]{:S(2)}, u32[]{:S(2)}) collective-permute-start(bf16[128,512]{1,0:T(8,128)(2,1)} %get-tuple-element.50), channel_id=1, source_target_pairs={{0,24},{8,16},{16,8},{24,0},{1,25},{9,17},{17,9},{25,1},{2,26},{10... | collective-permute-start | bytes 393224 | tf_op jit(solution)/shard_map/ppermute | solution.py:18
  9.5 9.1 %collective-permute-start.1 = (bf16[128,512]{1,0:T(8,128)(2,1)}, bf16[128,512]{1,0:T(8,128)(2,1)}, u32[]{:S(2)}, u32[]{:S(2)}) collective-permute-start(bf16[128,512]{1,0:T(8,128)(2,1)} %get-tuple-element.51), channel_id=1, source_target_pairs={{0,16},{8,24},{16,0},{24,8},{1,17},{9,25},{17,1},{25,9},{2,18},{10... | collective-permute-start | bytes 393224 | tf_op jit(solution)/shard_map/ppermute | solution.py:18
  11.2 1.2 collective-permute-start.4
  12.4 74.3 %collective-permute-start.7 = (bf16[128,512]{1,0:T(8,128)(2,1)}, bf16[128,512]{1,0:T(8,128)(2,1)S(1)}, u32[]{:S(2)}, u32[]{:S(2)}) collective-permute-start(bf16[128,512]{1,0:T(8,128)(2,1)} %get-tuple-element.46), channel_id=1, source_target_pairs={{0,24},{8,16},{16,8},{24,0},{1,25},{9,17},{17,9},{25,1},{2,26},{10... | collective-permute-start | bytes 393224 | tf_op jit(solution)/shard_map/ppermute | solution.py:18
  12.6 74.1 %collective-permute-start.6 = (bf16[128,512]{1,0:T(8,128)(2,1)}, bf16[128,512]{1,0:T(8,128)(2,1)S(1)}, u32[]{:S(2)}, u32[]{:S(2)}) collective-permute-start(bf16[128,512]{1,0:T(8,128)(2,1)} %get-tuple-element.47), channel_id=1, source_target_pairs={{0,16},{8,24},{16,0},{24,8},{1,17},{9,25},{17,1},{25,9},{2,18},{10... | collective-permute-start | bytes 393224 | tf_op jit(solution)/shard_map/ppermute | solution.py:18
  19.7 1.5 copy-start.1
  76.5 3.8 %copy-start.6 = (bf16[4,384,512]{2,1,0:T(8,128)(2,1)S(1)}, bf16[4,384,512]{2,1,0:T(8,128)(2,1)}, u32[]{:S(2)}) copy-start(bf16[4,384,512]{2,1,0:T(8,128)(2,1)} %param.15) | copy-start | bytes 4718596
  80.4 3.2 %copy-start.4 = (bf16[4,4,8,40,512]{4,3,0,2,1:T(8,128)(2,1)}, bf16[4,4,8,40,512]{4,3,0,2,1:T(8,128)(2,1)S(1)}, u32[]{:S(2)}) copy-start(bf16[4,4,8,40,512]{4,3,0,2,1:T(8,128)(2,1)S(1)} %convert_bitcast_fusion.1) | copy-start | bytes 15728644
  87.7 65.3 %slice-start = ((s8[7864320]{0:T(1024)(128)(4,1)}), s8[3670016]{0:T(1024)(128)(4,1)S(1)}, s32[]{:S(2)}) async-start(s8[7864320]{0:T(1024)(128)(4,1)} %bitcast.97), calls=%async_computation.1 | async-start | bytes 7340032
  146.8 6.2 %slice-start.1 = ((s8[7864320]{0:T(1024)(128)(4,1)}), s8[4194304]{0:T(1024)(128)(4,1)S(1)}, s32[]{:S(2)}) async-start(s8[7864320]{0:T(1024)(128)(4,1)} %bitcast.97), calls=%async_computation.2 | async-start | bytes 8388608
  153.0 2.1 copy-start.5
  154.2 8.3 %copy-start.2 = (bf16[4,4,8,40,384]{4,3,2,1,0:T(8,128)(2,1)}, bf16[4,4,8,40,384]{4,3,2,1,0:T(8,128)(2,1)S(1)}, u32[]{:S(2)}) copy-start(bf16[4,4,8,40,384]{4,3,2,1,0:T(8,128)(2,1)S(1)} %get-tuple-element.42) | copy-start | bytes 11796484
  154.2 8.2 %copy-start.3 = (bf16[4,4,8,40,384]{4,3,2,1,0:T(8,128)(2,1)}, bf16[4,4,8,40,384]{4,3,2,1,0:T(8,128)(2,1)S(1)}, u32[]{:S(2)}) copy-start(bf16[4,4,8,40,384]{4,3,2,1,0:T(8,128)(2,1)S(1)} %get-tuple-element.43) | copy-start | bytes 11796484
  163.6 103.3 %all-to-all-start = ((f32[8,4,128]{2,1,0:T(4,128)}), f32[8,4,128]{2,1,0:T(4,128)S(1)}, u32[]{:S(2)}, u32[]{:S(2)}) async-start(f32[8,4,128]{2,1,0:T(4,128)} %select_reduce_fusion.1), calls=%async_computation | async-start | bytes 32768 | tf_op jit(solution)/shard_map/all_to_all | solution.py:590

commit v4 on v3

--- a/solution.py
+++ b/solution.py
@@ -101,7 +101,49 @@
     def across(a, z_of, first, s, side):
         i, o = pairs[a]
         b = z_of * 2 + x
-        return remote(i if first else o.at[b], o.at[b], sems, (a, 2 + side, s), "expert", partner)
+        if first:
+            return remote(i, o.at[b], sems, (a, 2 + side, s), "expert", partner)
+        most = pl.ds(1, i.shape[0] - 1)
+        return remote(o.at[b, most], o.at[b, most], sems, (a, 2 + side, s), "expert", partner)
+
+    def crossed(a, b, side, s):
+        i, o = pairs[a]
+        most = pl.ds(1, i.shape[0] - 1)
+        return remote(i.at[most], o.at[b, most], sems, (a, 2 + side, s), "expert", partner)
+
+    def aside(a, side, s):
+        i, o = pairs[a]
+        b = (z - s if side == 0 else z + s) * 2 + 1 - x
+        return remote(o.at[b, 0], o.at[b, 0], sems, (a, 4 + side, s), "expert", j + 2 if side == 0 else j - 2)
+
+    def aside_landed(a, side, s):
+        i, o = pairs[a]
+        b = (z - 1 - s if side == 0 else z + 1 + s) * 2 + 1 - x
+        return remote(i.at[0], o.at[b, 0], sems, (a, 4 + side, s), "expert", partner)
+
+    def relay(s):
+        for a in range(len(pairs)):
+            if s < 0:
+                landed(a, partner, 2, 0).wait_recv()
+
+            for side in (0, 1):
+                more = (z < lines - 1) if side == 0 else (z > 0)
+                if s < 0:
+
+                    @pl.when(more)
+                    def _():
+                        aside(a, side, 0).start()
+
+                else:
+
+                    @pl.when((z - 1 - s >= 0) if side == 0 else (z + 1 + s < lines))
+                    def _():
+                        aside_landed(a, side, s).wait_recv()
+                        if s + 1 < lines - 1:
+
+                            @pl.when(more)
+                            def _():
+                                aside(a, side, s + 1).start()
 
     def landed(a, b, kind, s):
         i, o = pairs[a]
@@ -149,9 +191,16 @@
     def finish():
         for a, (i, o) in enumerate(pairs):
             pltpu.make_async_copy(i, o.at[j], local_sems.at[a]).wait()
-            landed(a, partner, 2, 0).wait_recv()
             across(a, z, True, 0, 0).wait_send()
             for s in range(lines - 1):
+
+                @pl.when((z - s >= 0) & (z < lines - 1))
+                def _():
+                    aside(a, 0, s).wait_send()
+
+                @pl.when((z + s < lines) & (z > 0))
+                def _():
+                    aside(a, 1, s).wait_send()
 
                 @pl.when((z - s >= 0) & (z < lines - 1))
                 def _():
@@ -164,16 +213,18 @@
                 @pl.when(z - 1 - s >= 0)
                 def _():
                     across(a, z - 1 - s, False, s + 1, 0).wait_send()
-                    landed(a, (z - 1 - s) * 2 + 1 - x, 2, s + 1).wait_recv()
+                    crossed(a, (z - 1 - s) * 2 + 1 - x, 0, s + 1).wait_recv()
 
                 @pl.when(z + 1 + s < lines)
                 def _():
                     across(a, z + 1 + s, False, s + 1, 1).wait_send()
-                    landed(a, (z + 1 + s) * 2 + 1 - x, 3, s + 1).wait_recv()
+                    crossed(a, (z + 1 + s) * 2 + 1 - x, 1, s + 1).wait_recv()
 
     todo.append(begin)
     for s in range(lines - 1):
         todo.append(functools.partial(step, s))
+        todo.append(functools.partial(relay, s - 1))
+    todo.append(functools.partial(relay, lines - 2))
     todo.append(finish)
     return todo
 
@@ -281,7 +332,7 @@
     for level in range(levels):
         for c in range(chunks):
             reduce(level, c)
-            if level == levels - 1 and c % 2 and rest:
+            if level == levels - 1 and c and rest:
                 rest.pop(0)()
     for level in range(1, gather_levels):
         for c in range(chunks):
@@ -315,7 +366,7 @@
         in_specs=[ANY] * 3,
         out_specs=[ANY] * 3,
         scratch_shapes=[
-            dma((2, 2, 4, lines)),
+            dma((2, 2, 6, lines)),
             dma((2,)),
             dma((2, bits, n_dp // 2, 2)),
             dma,
@@ -342,7 +393,7 @@
         in_specs=[ANY, VM],
         out_specs=[ANY, VM, VM],
         scratch_shapes=[
-            dma((2, 1, 4, lines)),
+            dma((2, 1, 6, lines)),
             dma((1,)),
             dma((2, bits, n_dp // 2, chunks)),
             dma((bits, 2, n_dp // 2, chunks)),

time: 269 us -> 271 us (level)
    pallas_call x1, Pallas kernels: 54 us -> 57 us  [gather_first(): pl.pallas_call(functools.partial(first_kernel, n_ex, n_dp), out_shape=(ja...]
  transfers between devices with their start and end apart: 9 -> 9, of which waited for: 3 -> 3; matrix products, arithmetic and copies ran while one was open for 20% -> 19% of each run, Pallas kernels for 43% -> 44%
where the time goes in v4:
time: 271 us; the launch traced here: 270 us
  Pallas kernels  176 us (65%)
  matrix products  43.9 us (16%)
  local copies, waits for them, and re-layouts  15.6 us (6%)
  other arithmetic  14.7 us (5%)
  starting transfers between devices  10.6 us (4%)
  waiting for transfers between devices  5.23 us (2%)
  between operations  3.95 us (1%)
    pallas_call x1, Pallas kernels, scatter_third(): pl.pallas_call(functools.partial(third_kernel, n_ex, n_dp), out_shape=(ja...  61.4 us
    pallas_call x1, Pallas kernels, gather_second(): pl.pallas_call(functools.partial(second_kernel, n_ex, n_dp, chunks), out_...  57.6 us
    pallas_call x1, Pallas kernels, gather_first(): pl.pallas_call(functools.partial(first_kernel, n_ex, n_dp), out_shape=(ja...  57 us
    dot_general x1, matrix products, body(): jnp.einsum('erjqd,rejqf->edf', xs, dgu, preferred_element_type=F32)  12.5 us
    dot_general x1, matrix products, body(): jnp.einsum('jreqt,erjqd->jrtd', pick, slot_grad, preferred_element_type=F32)  9.16 us
    dot_general x1, matrix products, body(): jnp.einsum('rejqf,erjqd->efd', hidden_p, gs, preferred_element_type=F32)  8.99 us
    another operation x1, other arithmetic  7.33 us
    ppermute x8, starting transfers between devices, xor_permute(): return lax.ppermute(x, axis, [(a, a ^ bit) for a in range(n)])  7.32 us
  transfers between devices with their start and end apart: 9, of which 3 were waited for; matrix products, arithmetic and copies ran while one was open for 19% of the time, Pallas kernels for 44%

profile of v4, /device:TPU:0, one launch (start us, length us, event | category | flops | bytes accessed | tf_op | source)
XLA Modules:
  0.0 270.1 jit_solution(17538425473873661859)
XLA Ops:
  0.6 0.8 convert_bitcast_fusion.4
  1.5 0.8 convert_bitcast_fusion.5
  2.3 3.0 %collective-permute-start.3 = (f32[1,16,128]{2,1,0:T(8,128)S(1)}, f32[1,16,128]{2,1,0:T(8,128)S(1)}, u32[]{:S(2)}, u32[]{:S(2)}) collective-permute-start(f32[1,16,128]{2,1,0:T(8,128)S(1)} %get-tuple-element.57), channel_id=1, source_target_pairs={{0,16},{8,24},{16,0},{24,8},{1,17},{9,25},{17,1},{25,9},{2,18},{10... | collective-permute-start | bytes 24584 | tf_op jit(solution)/shard_map/ppermute | solution.py:18
  5.3 1.9 dynamic-slice_bitcast_fusion
  7.2 1.8 dynamic-slice_bitcast_fusion.1
  9.5 1.6 collective-permute-start.1
  11.5 1.0 collective-permute-done.4
  12.6 1.7 collective-permute-start.6
  14.3 1.1 collective-permute-done.2
  15.4 3.2 %collective-permute-done.1 = bf16[128,512]{1,0:T(8,128)(2,1)} collective-permute-done((bf16[128,512]{1,0:T(8,128)(2,1)}, bf16[128,512]{1,0:T(8,128)(2,1)}, u32[]{:S(2)}, u32[]{:S(2)}) %collective-permute-start.1) | collective-permute-done | bytes 131104 | tf_op jit(solution)/shard_map/ppermute | solution.py:18
  18.6 1.1 pad_maximum_fusion.1.og
  19.7 1.5 copy-done.1
  21.3 57.0 %shard_map.119 = (bf16[8,4,128,512]{3,2,1,0:T(8,128)(2,1)}, f32[8,4,16,128]{3,2,1,0:T(8,128)S(1)}, bf16[4,1280,768]{2,1,0:T(8,128)(2,1)}) custom-call(bf16[4,128,512]{2,1,0:T(8,128)(2,1)S(1)} %pad_maximum_fusion.1.og, f32[4,16,128]{2,1,0:T(8,128)S(1)} %bitcast.95, bf16[1280,768]{1,0:T(8,128)(2,1)S(1)} %bitcast.93), custom_call_target="tpu_custom_call" | custom-call | tf_op jit(solution)/shard_map/pallas_call | solution.py:359
  79.5 3.8 %convert_bitcast_fusion.1 = bf16[4,4,8,40,512]{4,3,0,2,1:T(8,128)(2,1)S(1)} fusion(bf16[8,4,128,512]{3,2,1,0:T(8,128)(2,1)} %get-tuple-element.14, f32[8,4,4,128]{3,2,1,0:T(4,128)S(1)} %copy.57), kind=kOutput, calls=%fused_computation.28 | convolution fusion | flops 674365440 | bytes 9502720 | tf_op jit(solution)/shard_map/jreqt,jrtd->erjqd/dot_general | solution.py:618
  83.4 3.1 %convert_bitcast_fusion.2 = bf16[4,4,8,40,384]{4,3,2,0,1:T(8,128)(2,1)S(1)} fusion(bf16[4,4,8,40,512]{4,3,0,2,1:T(8,128)(2,1)S(1)} %convert_bitcast_fusion.1, bf16[4,384,512]{2,1,0:T(8,128)(2,1)S(1)} %copy-done.6), kind=kOutput, calls=%fused_computation.33 | convolution fusion | flops 2015232000 | bytes 10747904 | tf_op jit(solution)/shard_map/erjqd,efd->rejqf/dot_general | solution.py:619
  86.6 2.3 copy.61
  88.9 0.8 select_reduce_fusion
  89.7 1.0 pad_maximum_fusion.2.tk
  90.7 57.6 %shard_map.120 = (bf16[8,4,128,512]{3,2,1,0:T(8,128)(2,1)}, f32[1280,384]{1,0:T(8,128)S(1)}, bf16[4,1280,384]{2,1,0:T(8,128)(2,1)}) custom-call(bf16[4,128,512]{2,1,0:T(8,128)(2,1)S(1)} %pad_maximum_fusion.2.tk, bf16[4,1280,384]{2,1,0:T(8,128)(2,1)} %bitcast.96), custom_call_target="tpu_custom_call" | custom-call | tf_op jit(solution)/shard_map/pallas_call | solution.py:386
  148.3 6.1 %convert_bitcast_fusion = bf16[4,4,8,40,512]{4,3,1,2,0:T(8,128)(2,1)} fusion(bf16[8,4,128,512]{3,2,1,0:T(8,128)(2,1)} %get-tuple-element.17, f32[8,4,4,128]{3,2,1,0:T(4,128)S(1)} %copy.57), kind=kOutput, calls=%fused_computation.25 | convolution fusion | flops 674365440 | bytes 9502720 | tf_op jit(solution)/shard_map/jreqt,jrtd->erjqd/dot_general | solution.py:646
  154.5 1.2 fusion.58
  155.7 0.9 copy-done.5
  156.6 7.3 %fusion.2 = (bf16[4,4,8,40,384]{4,3,1,0,2:T(8,128)(2,1)}, bf16[4,4,8,40,384]{4,3,1,0,2:T(8,128)(2,1)}, f32[4,4,8,40,384]{4,3,1,0,2:T(8,128)S(1)}) fusion(f32[4,4,8,40]{3,1,0,2:T(4,128)S(1)} %bitcast.103, bf16[4,4,8,40,384]{4,3,2,1,0:T(8,128)(2,1)S(1)} %get-tuple-element.42, bf16[4,4,8,40,384]{4,3,2,1,0:T(8,128)(2,1)S(1)} %get-tuple-element.43, ...), kind=kLoop, calls=%fused_computation.8 | loop fusion | flops 35389440 | bytes 27545600 | tf_op jit(solution)/shard_map/convert.3
  164.3 0.9 select_reduce_fusion.1
  165.2 3.3 %all-to-all-start = ((f32[8,4,128]{2,1,0:T(4,128)}), f32[8,4,128]{2,1,0:T(4,128)S(1)}, u32[]{:S(2)}, u32[]{:S(2)}) async-start(f32[8,4,128]{2,1,0:T(4,128)} %select_reduce_fusion.1), calls=%async_computation | async-start | bytes 32768 | tf_op jit(solution)/shard_map/all_to_all | solution.py:641
  168.5 12.5 %multiply_reduce_fusion = (f32[]{:T(128)}, f32[4,512,768]{2,1,0:T(8,128)}) fusion(bf16[4,4,8,40,512]{4,3,1,2,0:T(8,128)(2,1)} %convert_bitcast_fusion, bf16[4,4,8,40,384]{4,3,1,0,2:T(8,128)(2,1)} %get-tuple-element.40, bf16[4,4,8,40,384]{4,3,1,0,2:T(8,128)(2,1)} %get-tuple-element.39), kind=kOutput, calls=%fused_computation.19 | convolution fusion | flops 4045406208 | bytes 19398660 | tf_op jit(solution)/shard_map/erjqd,rejqf->edf/dot_general | solution.py:648
  181.0 9.2 %bitcast_convert_fusion.tok = bf16[8,4,128,512]{3,2,1,0:T(8,128)(2,1)} fusion(bf16[4,512,768]{2,1,0:T(8,128)(2,1)S(1)} %copy-done, f32[8,4,4,128]{3,2,1,0:T(4,128)S(1)} %copy.57, bf16[4,4,8,40,384]{4,3,1,0,2:T(8,128)(2,1)} %get-tuple-element.40, bf16[4,4,8,40,384]{4,3,1,0,2:T(8,128)(2,1)} %get-tuple-element.39), kind=kOutput, calls=%fused_computation.5 | convolution fusion | flops 4718723072 | bytes 15269888 | tf_op jit(solution)/shard_map/jreqt,erjqd->jrtd/dot_general | solution.py:637
  190.2 9.0 %multiply_reduce_fusion.1 = (f32[]{:T(128)}, f32[4,384,512]{2,1,0:T(8,128)}) fusion(bf16[4,4,8,40,512]{4,3,0,2,1:T(8,128)(2,1)} %copy-done.4, f32[4,4,8,40]{3,1,0,2:T(4,128)S(1)} %bitcast.104, bf16[4,4,8,40,384]{4,3,2,1,0:T(8,128)(2,1)} %copy-done.2, bf16[4,4,8,40,384]{4,3,2,1,0:T(8,128)(2,1)} %copy-done.3), kind=kOutput, calls=%fused_computation.37 | convolution fusion | flops 2032533504 | bytes 16273412 | tf_op jit(solution)/shard_map/rejqf,erjqd->efd/dot_general | solution.py:647
  201.0 61.4 %shard_map.121 = (bf16[4,128,512]{2,1,0:T(8,128)(2,1)}, f32[8,128]{1,0:T(8,128)}) custom-call(bf16[8,4,128,512]{3,2,1,0:T(8,128)(2,1)} %bitcast_convert_fusion.tok, f32[8,128]{1,0:T(8,128)} %broadcast_in_dim.64.square), custom_call_target="tpu_custom_call" | custom-call | tf_op jit(solution)/shard_map/pallas_call | solution.py:551
  262.4 1.2 slice.27
  263.6 2.0 copy.69
  265.6 2.0 copy.73
  (45 shorter events, 3.9 us)
Async XLA Ops:
  0.6 180.4 %copy-start = (bf16[4,512,768]{2,1,0:T(8,128)(2,1)S(1)}, bf16[4,512,768]{2,1,0:T(8,128)(2,1)}, u32[]{:S(2)}) copy-start(bf16[4,512,768]{2,1,0:T(8,128)(2,1)} %param.14) | copy-start | bytes 9437188
  2.3 8.8 %collective-permute-start.3 = (f32[1,16,128]{2,1,0:T(8,128)S(1)}, f32[1,16,128]{2,1,0:T(8,128)S(1)}, u32[]{:S(2)}, u32[]{:S(2)}) collective-permute-start(f32[1,16,128]{2,1,0:T(8,128)S(1)} %get-tuple-element.57), channel_id=1, source_target_pairs={{0,16},{8,24},{16,0},{24,8},{1,17},{9,25},{17,1},{25,9},{2,18},{10... | collective-permute-start | bytes 24584 | tf_op jit(solution)/shard_map/ppermute | solution.py:18
  7.2 82.5 %collective-permute-start.5 = (bf16[128,512]{1,0:T(8,128)(2,1)}, bf16[128,512]{1,0:T(8,128)(2,1)}, u32[]{:S(2)}, u32[]{:S(2)}) collective-permute-start(bf16[128,512]{1,0:T(8,128)(2,1)} %get-tuple-element.45), channel_id=1, source_target_pairs={{0,8},{8,0},{16,24},{24,16},{1,9},{9,1},{17,25},{25,17},{2,10},{10... | collective-permute-start | bytes 393224 | tf_op jit(solution)/shard_map/ppermute | solution.py:18
  9.0 3.6 %collective-permute-start = (bf16[128,512]{1,0:T(8,128)(2,1)}, bf16[128,512]{1,0:T(8,128)(2,1)}, u32[]{:S(2)}, u32[]{:S(2)}) collective-permute-start(bf16[128,512]{1,0:T(8,128)(2,1)} %get-tuple-element.49), channel_id=1, source_target_pairs={{0,8},{8,0},{16,24},{24,16},{1,9},{9,1},{17,25},{25,17},{2,10},{10... | collective-permute-start | bytes 393224 | tf_op jit(solution)/shard_map/ppermute | solution.py:18
  9.5 5.9 %collective-permute-start.2 = (bf16[128,512]{1,0:T(8,128)(2,1)}, bf16[128,512]{1,0:T(8,128)(2,1)}, u32[]{:S(2)}, u32[]{:S(2)}) collective-permute-start(bf16[128,512]{1,0:T(8,128)(2,1)} %get-tuple-element.50), channel_id=1, source_target_pairs={{0,24},{8,16},{16,8},{24,0},{1,25},{9,17},{17,9},{25,1},{2,26},{10... | collective-permute-start | bytes 393224 | tf_op jit(solution)/shard_map/ppermute | solution.py:18
  9.5 9.1 %collective-permute-start.1 = (bf16[128,512]{1,0:T(8,128)(2,1)}, bf16[128,512]{1,0:T(8,128)(2,1)}, u32[]{:S(2)}, u32[]{:S(2)}) collective-permute-start(bf16[128,512]{1,0:T(8,128)(2,1)} %get-tuple-element.51), channel_id=1, source_target_pairs={{0,16},{8,24},{16,0},{24,8},{1,17},{9,25},{17,1},{25,9},{2,18},{10... | collective-permute-start | bytes 393224 | tf_op jit(solution)/shard_map/ppermute | solution.py:18
  11.2 1.2 collective-permute-start.4
  12.4 77.3 %collective-permute-start.7 = (bf16[128,512]{1,0:T(8,128)(2,1)}, bf16[128,512]{1,0:T(8,128)(2,1)S(1)}, u32[]{:S(2)}, u32[]{:S(2)}) collective-permute-start(bf16[128,512]{1,0:T(8,128)(2,1)} %get-tuple-element.46), channel_id=1, source_target_pairs={{0,24},{8,16},{16,8},{24,0},{1,25},{9,17},{17,9},{25,1},{2,26},{10... | collective-permute-start | bytes 393224 | tf_op jit(solution)/shard_map/ppermute | solution.py:18
  12.6 77.1 %collective-permute-start.6 = (bf16[128,512]{1,0:T(8,128)(2,1)}, bf16[128,512]{1,0:T(8,128)(2,1)S(1)}, u32[]{:S(2)}, u32[]{:S(2)}) collective-permute-start(bf16[128,512]{1,0:T(8,128)(2,1)} %get-tuple-element.47), channel_id=1, source_target_pairs={{0,16},{8,24},{16,0},{24,8},{1,17},{9,25},{17,1},{25,9},{2,18},{10... | collective-permute-start | bytes 393224 | tf_op jit(solution)/shard_map/ppermute | solution.py:18
  19.7 1.5 copy-start.1
  79.5 3.8 %copy-start.6 = (bf16[4,384,512]{2,1,0:T(8,128)(2,1)S(1)}, bf16[4,384,512]{2,1,0:T(8,128)(2,1)}, u32[]{:S(2)}) copy-start(bf16[4,384,512]{2,1,0:T(8,128)(2,1)} %param.15) | copy-start | bytes 4718596
  83.4 3.2 %copy-start.4 = (bf16[4,4,8,40,512]{4,3,0,2,1:T(8,128)(2,1)}, bf16[4,4,8,40,512]{4,3,0,2,1:T(8,128)(2,1)S(1)}, u32[]{:S(2)}) copy-start(bf16[4,4,8,40,512]{4,3,0,2,1:T(8,128)(2,1)S(1)} %convert_bitcast_fusion.1) | copy-start | bytes 15728644
  90.7 63.8 %slice-start = ((s8[7864320]{0:T(1024)(128)(4,1)}), s8[3670016]{0:T(1024)(128)(4,1)S(1)}, s32[]{:S(2)}) async-start(s8[7864320]{0:T(1024)(128)(4,1)} %bitcast.97), calls=%async_computation.1 | async-start | bytes 7340032
  148.3 6.2 %slice-start.1 = ((s8[7864320]{0:T(1024)(128)(4,1)}), s8[4194304]{0:T(1024)(128)(4,1)S(1)}, s32[]{:S(2)}) async-start(s8[7864320]{0:T(1024)(128)(4,1)} %bitcast.97), calls=%async_computation.2 | async-start | bytes 8388608
  154.5 2.1 copy-start.5
  155.7 8.3 %copy-start.2 = (bf16[4,4,8,40,384]{4,3,2,1,0:T(8,128)(2,1)}, bf16[4,4,8,40,384]{4,3,2,1,0:T(8,128)(2,1)S(1)}, u32[]{:S(2)}) copy-start(bf16[4,4,8,40,384]{4,3,2,1,0:T(8,128)(2,1)S(1)} %get-tuple-element.42) | copy-start | bytes 11796484
  155.7 8.2 %copy-start.3 = (bf16[4,4,8,40,384]{4,3,2,1,0:T(8,128)(2,1)}, bf16[4,4,8,40,384]{4,3,2,1,0:T(8,128)(2,1)S(1)}, u32[]{:S(2)}) copy-start(bf16[4,4,8,40,384]{4,3,2,1,0:T(8,128)(2,1)S(1)} %get-tuple-element.43) | copy-start | bytes 11796484
  165.2 103.2 %all-to-all-start = ((f32[8,4,128]{2,1,0:T(4,128)}), f32[8,4,128]{2,1,0:T(4,128)S(1)}, u32[]{:S(2)}, u32[]{:S(2)}) async-start(f32[8,4,128]{2,1,0:T(4,128)} %select_reduce_fusion.1), calls=%async_computation | async-start | bytes 32768 | tf_op jit(solution)/shard_map/all_to_all | solution.py:641
